TPU v7x, 256 devices: a whole 4x4x8 slice. The times are simulated.
256 devices in a mesh: gx: 32 (over x, z_hi, core), gy: 8 (over y, z_lo).
Axes of the slice: x: 4, y: 4, z: 8 (z_hi: 4, z_lo: 2; z = z_hi * 2 + z_lo), core: 2. Of those that a mesh axis runs over, the one named last changes fastest.
Arguments:
- flow_state: float32 [5, 2, 512, 4096], P(None, None, 'gx', 'gy'), may hold values from -1 to 5
- colour_map: int32 [2, 512, 4096], P(None, 'gx', 'gy'), may hold values from 0 to 26
- cell_flags: int32 [512, 4096], P('gx', 'gy'), may hold values 0 or 1
- probe_weights: float32 [2, 27, 5], replicated, may hold values from -6 to 6
Outputs:
- tangent_residual: float32 [2, 5, 2, 512, 4096], P(None, None, None, 'gx', 'gy')
All inputs are finite; a program needn't handle non-finite values. No bound on the sum of `cell_flags` on one device may be relied on, other than what follows from the above.
Results may differ from a plain program's by a relative error of at most 0.0003.
Values sent between devices are 32-bit elements; how exact they have to be, the bound alone decides.
No kernel may reach another device: no remote copies, remote signals or barrier semaphores. Data moves between devices by JAX's collectives and lax.ppermute only.
A program may use at most 64 MiB of HBM per device.

v0:
```python
import jax
import jax.numpy as jnp
from jax import lax
from jax.sharding import PartitionSpec as P

GAMMA = 1.4
VISCOSITY = 0.2
CONDUCT = 0.2 * 1.4 / (0.4 * 0.72)
DISSIPATE = 0.5


def with_halo(cells, sides, width):
    for axis, dim in sides:
        count = lax.axis_size(axis)
        head = lax.slice_in_dim(cells, 0, width, axis=dim)
        tail = lax.slice_in_dim(cells, cells.shape[dim] - width, cells.shape[dim], axis=dim)
        cells = jnp.concatenate(
            [
                lax.ppermute(tail, axis, [(i, (i + 1) % count) for i in range(count)]),
                cells,
                lax.ppermute(head, axis, [((i + 1) % count, i) for i in range(count)]),
            ],
            axis=dim,
        )
    return cells


def pair_list(facing):
    chosen = []
    for entry_pair in [
        (0, facing),
        (1, facing),
        (2, facing),
        (facing, 0),
        (facing, 1),
        (facing, 2),
        (0, 0),
        (1, 1),
        (2, 2),
        (3, facing),
    ]:
        if entry_pair not in chosen:
            chosen.append(entry_pair)
    return chosen


def trim_axis(values, start, trim, from_end):
    axis_number = values.ndim - from_end
    return lax.slice_in_dim(values, start, values.shape[axis_number] - trim, axis=axis_number)


def basic_unknowns(grid_tensor_list):
    specific_weight_per_volume = grid_tensor_list[0]
    fluid_motion_vector = grid_tensor_list[1:4] / specific_weight_per_volume
    kinetic = 0.5 * jnp.sum(grid_tensor_list[1:4] * fluid_motion_vector, axis=0)
    normal_stress_scalar = (GAMMA - 1.0) * (grid_tensor_list[4] - kinetic)
    thermal_level = normal_stress_scalar / specific_weight_per_volume
    return (specific_weight_per_volume, fluid_motion_vector, normal_stress_scalar, thermal_level)


def level_grad(grid_tensor_list):
    levels = grid_tensor_list.shape[-3]
    level_above = jnp.concatenate(
        [grid_tensor_list[..., 1:, :, :], grid_tensor_list[..., -1:, :, :]], axis=-3
    )
    level_below = jnp.concatenate(
        [grid_tensor_list[..., :1, :, :], grid_tensor_list[..., :-1, :, :]], axis=-3
    )
    position = jnp.arange(levels)
    factor = jnp.where((position == 0) | (position == levels - 1), 1.0, 0.5).astype(
        grid_tensor_list.dtype
    )
    return (level_above - level_below) * factor[:, None, None]


def gradients(extended_solution):
    specific_weight_per_volume, fluid_motion_vector, normal_stress_scalar, thermal_level = (
        basic_unknowns(extended_solution)
    )
    physical_measure = jnp.concatenate([fluid_motion_vector, thermal_level[None]], axis=0)
    along_x = 0.5 * (physical_measure[:, :, 2:, 1:-1] - physical_measure[:, :, :-2, 1:-1])
    along_y = 0.5 * (physical_measure[:, :, 1:-1, 2:] - physical_measure[:, :, 1:-1, :-2])
    along_z = level_grad(physical_measure)[:, :, 1:-1, 1:-1]
    return jnp.stack([along_x, along_y, along_z], axis=1)


def pick_components(gradient_set, facing):
    return jnp.stack(
        [gradient_set[entry_pair[0], entry_pair[1]] for entry_pair in pair_list(facing)]
    )


def viscous_face(facing, comps_low, comps_high, vel_low, vel_high):
    chosen = pair_list(facing)

    def face_grad(variable, towards):
        position = chosen.index((variable, towards))
        return 0.5 * (comps_low[position] + comps_high[position])

    vel_face = 0.5 * (vel_low + vel_high)
    diverge = face_grad(0, 0) + face_grad(1, 1) + face_grad(2, 2)
    stresses = []
    for component in range(3):
        stress_term = VISCOSITY * (face_grad(component, facing) + face_grad(facing, component))
        if component == facing:
            stress_term = stress_term - 2.0 / 3.0 * VISCOSITY * diverge
        stresses.append(stress_term)
    energy = vel_face[0] * stresses[0] + vel_face[1] * stresses[1] + vel_face[2] * stresses[2]
    energy = energy + CONDUCT * face_grad(3, facing)
    return jnp.stack([jnp.zeros_like(energy), stresses[0], stresses[1], stresses[2], energy])


def inviscid_flux(grid_tensor_list, facing):
    specific_weight_per_volume, fluid_motion_vector, normal_stress_scalar, thermal_level = (
        basic_unknowns(grid_tensor_list)
    )
    normal_vel = fluid_motion_vector[facing]
    momenta = []
    for component in range(3):
        momentum_flux = grid_tensor_list[1 + component] * normal_vel
        if component == facing:
            momentum_flux = momentum_flux + normal_stress_scalar
        momenta.append(momentum_flux)
    fluxes = jnp.stack(
        [
            grid_tensor_list[1 + facing],
            momenta[0],
            momenta[1],
            momenta[2],
            (grid_tensor_list[4] + normal_stress_scalar) * normal_vel,
        ]
    )
    speeds = jnp.sqrt(
        normal_vel * normal_vel + GAMMA * normal_stress_scalar / specific_weight_per_volume
    )
    return (fluxes, speeds, fluid_motion_vector)


def direction_divergence(strip, comps, facing):
    from_end = 2 if facing == 0 else 1
    fluxes, speeds, fluid_motion_vector = inviscid_flux(strip, facing)
    central = (
        7.0 * (trim_axis(fluxes, 1, 2, from_end) + trim_axis(fluxes, 2, 1, from_end))
        - (trim_axis(fluxes, 0, 3, from_end) + trim_axis(fluxes, 3, 0, from_end))
    ) / 12.0
    state_jump = trim_axis(strip, 2, 1, from_end) - trim_axis(strip, 1, 2, from_end)
    central = (
        central
        - DISSIPATE
        * 0.5
        * (trim_axis(speeds, 1, 2, from_end) + trim_axis(speeds, 2, 1, from_end))
        * state_jump
    )
    viscous = viscous_face(
        facing,
        trim_axis(comps, 0, 1, from_end),
        trim_axis(comps, 1, 0, from_end),
        trim_axis(fluid_motion_vector, 1, 2, from_end),
        trim_axis(fluid_motion_vector, 2, 1, from_end),
    )
    face_sum = central - viscous
    return trim_axis(face_sum, 1, 0, from_end) - trim_axis(face_sum, 0, 1, from_end)


def level_divergence(inner_state, gradient_set):
    fluxes, speeds, fluid_motion_vector = inviscid_flux(inner_state, 2)
    central = 0.5 * (fluxes[:, :-1] + fluxes[:, 1:])
    central = central - DISSIPATE * 0.5 * (speeds[:-1] + speeds[1:]) * (
        inner_state[:, 1:] - inner_state[:, :-1]
    )
    comps = pick_components(gradient_set, 2)
    viscous = viscous_face(
        2, comps[:, :-1], comps[:, 1:], fluid_motion_vector[:, :-1], fluid_motion_vector[:, 1:]
    )
    face_sum = central - viscous
    wall_zero = jnp.zeros_like(face_sum[:, :1])
    padded_faces = jnp.concatenate([wall_zero, face_sum, wall_zero], axis=1)
    return padded_faces[:, 1:] - padded_faces[:, :-1]


def assemble(extended_solution, comps_x, comps_y, gradient_set):
    strip_x = extended_solution[:, :, :, 2:-2]
    strip_y = extended_solution[:, :, 2:-2, :]
    inner_state = extended_solution[:, :, 2:-2, 2:-2]
    return -(
        direction_divergence(strip_x, comps_x, 0)
        + direction_divergence(strip_y, comps_y, 1)
        + level_divergence(inner_state, gradient_set)
    )


def make_seeds(tinted, probe_weights):
    palette = jnp.arange(probe_weights.shape[1], dtype=jnp.int32)
    onehot = (tinted[None] == palette[:, None, None, None]).astype(probe_weights.dtype)
    return jnp.einsum("pcv,clxy->pvlxy", probe_weights, onehot, precision=lax.Precision.HIGHEST)


def first_section(grid_tensor_list):
    gradient_set = gradients(grid_tensor_list)
    return (gradient_set, pick_components(gradient_set, 0), pick_components(gradient_set, 1))


def local(flow_state, colour_map, cell_flags, probe_weights):
    probe_count = probe_weights.shape[0]
    variable_count = flow_state.shape[0]
    local_seeds = make_seeds(colour_map, probe_weights)
    packed = jnp.concatenate(
        [flow_state, local_seeds.reshape((-1,) + flow_state.shape[1:])], axis=0
    )
    joined = with_halo(packed, (("gx", 2), ("gy", 3)), 2)
    extended_solution = joined[:variable_count]
    seed_field = joined[variable_count:].reshape((probe_count, variable_count) + joined.shape[1:])
    inner_pad = extended_solution[:, :, 1:-1, 1:-1]
    inner_seeds = seed_field[:, :, :, 1:-1, 1:-1]

    def gradient_probe(probe_seed):
        return jax.jvp(first_section, (inner_pad,), (probe_seed,))

    primal_parts, tangent_parts = jax.vmap(gradient_probe, out_axes=(None, 0))(inner_seeds)
    gradient_set, along_x, along_y = primal_parts
    grad_tangents, tangent_x, tangent_y = tangent_parts
    stack_x = jnp.concatenate([along_x[None], tangent_x], axis=0)
    stack_y = jnp.concatenate([along_y[None], tangent_y], axis=0)
    rim_x = with_halo(stack_x.reshape((-1,) + along_x.shape[1:]), (("gx", 2),), 1)
    rim_y = with_halo(stack_y.reshape((-1,) + along_y.shape[1:]), (("gy", 3),), 1)
    rim_x = rim_x.reshape(stack_x.shape[:2] + rim_x.shape[1:])
    rim_y = rim_y.reshape(stack_y.shape[:2] + rim_y.shape[1:])

    def residual_probe(probe_seed, seed_x, seed_y, seed_grad):
        return jax.jvp(
            assemble,
            (extended_solution, rim_x[0], rim_y[0], gradient_set),
            (probe_seed, seed_x, seed_y, seed_grad),
        )

    primal_out, tangents = jax.vmap(residual_probe, out_axes=(None, 0))(
        seed_field, rim_x[1:], rim_y[1:], grad_tangents
    )
    solid_mask = (cell_flags == 1)[None, None, None]
    return jnp.where(solid_mask, -seed_field[:, :, :, 2:-2, 2:-2], tangents)


def solution(mesh):
    placed = (P(None, None, "gx", "gy"), P(None, "gx", "gy"), P("gx", "gy"), P())
    return jax.shard_map(
        local,
        mesh=mesh,
        in_specs=placed,
        out_specs=P(None, None, None, "gx", "gy"),
        check_vma=False,
    )
```

profile of v0, /device:TPU:32, one launch (start us, length us, event | category | flops | bytes accessed | tf_op | source)
XLA Modules:
  0.0 70.8 jit_solution(10360297384510060116)
XLA Ops:
  0.0 0.7 copy-done
  0.7 1.9 %fusion.3 = f32[2,5,2,16,512]{4,1,0,3,2:T(8,128)S(1)} fusion(s32[2,16,512]{2,1,0:T(8,128)} %param.5, f32[2,27,5,1,1]{1,0,2,4,3:T(2,128)S(1)} %bitcast.521), kind=kOutput, calls=%fused_computation.14 | convolution fusion | flops 53526528 | bytes 721976 | tf_op jit(solution)/shard_map/pcv,clxy->pvlxy/dot_general | solution.py:195
  2.6 0.4 copy.40
  3.2 7.1 %collective-permute-start.1 = (f32[15,2,2,512]{3,2,1,0:T(2,128)S(1)}, f32[15,2,2,512]{3,2,1,0:T(2,128)S(1)}, u32[]{:S(2)}, u32[]{:S(2)}) collective-permute-start(f32[15,2,2,512]{3,2,1,0:T(2,128)S(1)} %get-tuple-element.128), channel_id=1, source_target_pairs={{8,0},{16,8},{24,16},{32,24},{40,32},{48,40},{56,48},{64,56},{72,6... | collective-permute-start | bytes 368648 | tf_op jit(solution)/shard_map/ppermute | solution.py:21
  10.6 0.5 copy-done.2
  11.1 3.0 %collective-permute-done = f32[15,2,2,512]{3,2,1,0:T(2,128)S(1)} collective-permute-done((f32[15,2,2,512]{3,2,1,0:T(2,128)S(1)}, f32[15,2,2,512]{3,2,1,0:T(2,128)S(1)}, u32[]{:S(2)}, u32[]{:S(2)}) %collective-permute-start) | collective-permute-done | bytes 122912 | tf_op jit(solution)/shard_map/ppermute | solution.py:19
  14.1 0.3 pad_maximum_fusion.5
  15.0 2.1 %collective-permute-start.2 = (f32[15,2,20,2]{3,2,1,0:T(8,128)S(1)}, f32[15,2,20,2]{3,2,1,0:T(8,128)S(1)}, u32[]{:S(2)}, u32[]{:S(2)}) collective-permute-start(f32[15,2,20,2]{3,2,1,0:T(8,128)S(1)} %get-tuple-element.75), channel_id=1, source_target_pairs={{0,1},{1,2},{2,3},{3,4},{4,5},{5,6},{6,7},{7,0},{8,9},{9,10},{10,1... | collective-permute-start | bytes 14408 | tf_op jit(solution)/shard_map/ppermute | solution.py:19
  17.2 9.3 %collective-permute-done.2 = f32[15,2,20,2]{3,2,1,0:T(8,128)S(1)} collective-permute-done((f32[15,2,20,2]{3,2,1,0:T(8,128)S(1)}, f32[15,2,20,2]{3,2,1,0:T(8,128)S(1)}, u32[]{:S(2)}, u32[]{:S(2)}) %collective-permute-start.2) | collective-permute-done | bytes 4832 | tf_op jit(solution)/shard_map/ppermute | solution.py:19
  26.6 5.8 %collective-permute-done.3 = f32[15,2,20,2]{3,2,1,0:T(8,128)S(1)} collective-permute-done((f32[15,2,20,2]{3,2,1,0:T(8,128)S(1)}, f32[15,2,20,2]{3,2,1,0:T(8,128)S(1)}, u32[]{:S(2)}, u32[]{:S(2)}) %collective-permute-start.3) | collective-permute-done | bytes 4832 | tf_op jit(solution)/shard_map/ppermute | solution.py:21
  32.4 1.1 %pad_maximum_fusion = f32[15,2,20,516]{3,2,1,0:T(8,128)S(1)} fusion(f32[15,2,20,2]{3,2,1,0:T(8,128)S(1)} %collective-permute-done.3, f32[15,2,2,512]{3,2,1,0:T(2,128)S(1)} %collective-permute-done.1, f32[10,2,16,512]{3,2,1,0:T(8,128)S(1)} %bitcast.539, f32[5,2,16,512]{3,2,1,0:T(8,128)S(1)} %copy-done.1, f32[15,2,2,512]{3,2,1,0:T(2,128)S(1)} %collective-permute-done, ...), kind=kLoop, calls=%fused_computation.8 | loop fusion | flops 1548000 | bytes 2476800 | tf_op jit(solution)/shard_map/concatenate | solution.py:17
  34.4 0.3 add_reduce_fusion
  35.1 0.5 fusion.31
  35.6 0.3 fusion.54
  36.2 0.3 fusion.278
  36.5 0.7 fusion.277
  38.0 0.5 fusion.279
  38.5 0.4 fusion.39
  41.4 6.0 %collective-permute-start.5 = (f32[24,2,1,512]{3,2,1,0:T(1,128)S(1)}, f32[24,2,1,512]{3,2,1,0:T(1,128)S(1)}, u32[]{:S(2)}, u32[]{:S(2)}) collective-permute-start(f32[24,2,1,512]{3,2,1,0:T(1,128)S(1)} %get-tuple-element.71), channel_id=1, source_target_pairs={{8,0},{16,8},{24,16},{32,24},{40,32},{48,40},{56,48},{64,56},{72,6... | collective-permute-start | bytes 294920 | tf_op jit(solution)/shard_map/ppermute | solution.py:21
  47.6 0.3 fusion.41
  48.9 0.9 %collective-permute-start.6 = (f32[24,2,16,1]{3,2,1,0:T(8,128)S(1)}, f32[24,2,16,1]{3,2,1,0:T(8,128)S(1)}, u32[]{:S(2)}, u32[]{:S(2)}) collective-permute-start(f32[24,2,16,1]{3,2,1,0:T(8,128)S(1)} %get-tuple-element.72), channel_id=1, source_target_pairs={{0,1},{1,2},{2,3},{3,4},{4,5},{5,6},{6,7},{7,0},{8,9},{9,10},{10,1... | collective-permute-start | bytes 9224 | tf_op jit(solution)/shard_map/ppermute | solution.py:19
  49.8 1.2 %collective-permute-start.7 = (f32[24,2,16,1]{3,2,1,0:T(8,128)S(1)}, f32[24,2,16,1]{3,2,1,0:T(8,128)S(1)}, u32[]{:S(2)}, u32[]{:S(2)}) collective-permute-start(f32[24,2,16,1]{3,2,1,0:T(8,128)S(1)} %get-tuple-element.73), channel_id=1, source_target_pairs={{1,0},{2,1},{3,2},{4,3},{5,4},{6,5},{7,6},{0,7},{9,8},{10,9},{11,1... | collective-permute-start | bytes 9224 | tf_op jit(solution)/shard_map/ppermute | solution.py:21
  52.3 7.6 %collective-permute-done.6 = f32[24,2,16,1]{3,2,1,0:T(8,128)S(1)} collective-permute-done((f32[24,2,16,1]{3,2,1,0:T(8,128)S(1)}, f32[24,2,16,1]{3,2,1,0:T(8,128)S(1)}, u32[]{:S(2)}, u32[]{:S(2)}) %collective-permute-start.6) | collective-permute-done | bytes 3104 | tf_op jit(solution)/shard_map/ppermute | solution.py:19
  59.9 5.2 %collective-permute-done.7 = f32[24,2,16,1]{3,2,1,0:T(8,128)S(1)} collective-permute-done((f32[24,2,16,1]{3,2,1,0:T(8,128)S(1)}, f32[24,2,16,1]{3,2,1,0:T(8,128)S(1)}, u32[]{:S(2)}, u32[]{:S(2)}) %collective-permute-start.7) | collective-permute-done | bytes 3104 | tf_op jit(solution)/shard_map/ppermute | solution.py:21
  65.1 0.5 pad_maximum_fusion.6
  65.6 0.4 fusion.274
  66.7 0.7 %fusion.19 = f32[2,5,2,16,513]{4,3,0,2,1:T(8,128)S(1)} fusion(f32[2,5,2,16,513]{4,3,0,2,1:T(8,128)S(1)} %fusion.108, f32[5,2,2,16,516]{4,3,1,2,0:T(8,128)S(1)} %fusion.138, f32[2,5,2,16,513]{4,3,2,1,0:T(8,128)S(1)} %get-tuple-element.113, f32[2,5,2,16,513]{4,3,2,1,0:T(8,128)S(1)} %get-tuple-element.112, f32[2,16,513]{2,1,0:T(8,128)S(1)} %fusion.210, ...), kind=kLoop, calls=%fused_computation.44 | loop fusion | flops 1805760 | bytes 5778432 | tf_op jit(solution)/shard_map/vmap(jvp())/sub | solution.py:161
  67.4 0.3 pad_maximum_fusion.1
  67.8 0.3 fusion.270
  68.8 0.7 fusion.11
  69.5 0.5 fusion.26
  69.9 0.9 %copy.114 = f32[2,5,2,16,512]{4,3,2,1,0:T(8,128)} copy(f32[2,5,2,16,512]{4,3,0,2,1:T(8,128)S(1)} %fusion.26) | data formatting | bytes 1310720 | tf_op jit(solution)/shard_map/jit(_where)/select_n | solution.py:240
  (136 shorter events, 9.3 us)
Async XLA Ops:
  0.0 0.7 copy-start
  0.0 3.0 %copy-start.1 = (f32[5,2,16,512]{3,2,1,0:T(8,128)S(1)}, f32[5,2,16,512]{3,2,1,0:T(8,128)}, u32[]{:S(2)}) copy-start(f32[5,2,16,512]{3,2,1,0:T(8,128)} %param.4) | copy-start | bytes 983044
  3.1 11.0 %collective-permute-start = (f32[15,2,2,512]{3,2,1,0:T(2,128)S(1)}, f32[15,2,2,512]{3,2,1,0:T(2,128)S(1)}, u32[]{:S(2)}, u32[]{:S(2)}) collective-permute-start(f32[15,2,2,512]{3,2,1,0:T(2,128)S(1)} %get-tuple-element.127), channel_id=1, source_target_pairs={{0,8},{8,16},{16,24},{24,32},{32,40},{40,48},{48,56},{56,64},{64,7... | collective-permute-start | bytes 368648 | tf_op jit(solution)/shard_map/ppermute | solution.py:19
  3.2 10.9 %collective-permute-start.1 = (f32[15,2,2,512]{3,2,1,0:T(2,128)S(1)}, f32[15,2,2,512]{3,2,1,0:T(2,128)S(1)}, u32[]{:S(2)}, u32[]{:S(2)}) collective-permute-start(f32[15,2,2,512]{3,2,1,0:T(2,128)S(1)} %get-tuple-element.128), channel_id=1, source_target_pairs={{8,0},{16,8},{24,16},{32,24},{40,32},{48,40},{56,48},{64,56},{72,6... | collective-permute-start | bytes 368648 | tf_op jit(solution)/shard_map/ppermute | solution.py:21
  10.3 0.8 %copy-start.2 = (s32[16,512]{1,0:T(8,128)S(1)}, s32[16,512]{1,0:T(8,128)}, u32[]{:S(2)}) copy-start(s32[16,512]{1,0:T(8,128)} %param.6) | copy-start | bytes 98308
  15.0 11.6 %collective-permute-start.2 = (f32[15,2,20,2]{3,2,1,0:T(8,128)S(1)}, f32[15,2,20,2]{3,2,1,0:T(8,128)S(1)}, u32[]{:S(2)}, u32[]{:S(2)}) collective-permute-start(f32[15,2,20,2]{3,2,1,0:T(8,128)S(1)} %get-tuple-element.75), channel_id=1, source_target_pairs={{0,1},{1,2},{2,3},{3,4},{4,5},{5,6},{6,7},{7,0},{8,9},{9,10},{10,1... | collective-permute-start | bytes 14408 | tf_op jit(solution)/shard_map/ppermute | solution.py:19
  17.0 15.4 %collective-permute-start.3 = (f32[15,2,20,2]{3,2,1,0:T(8,128)S(1)}, f32[15,2,20,2]{3,2,1,0:T(8,128)S(1)}, u32[]{:S(2)}, u32[]{:S(2)}) collective-permute-start(f32[15,2,20,2]{3,2,1,0:T(8,128)S(1)} %get-tuple-element.76), channel_id=1, source_target_pairs={{1,0},{2,1},{3,2},{4,3},{5,4},{6,5},{7,6},{0,7},{9,8},{10,9},{11,1... | collective-permute-start | bytes 14408 | tf_op jit(solution)/shard_map/ppermute | solution.py:21
  41.3 26.1 %collective-permute-start.4 = (f32[24,2,1,512]{3,2,1,0:T(1,128)S(1)}, f32[24,2,1,512]{3,2,1,0:T(1,128)S(1)}, u32[]{:S(2)}, u32[]{:S(2)}) collective-permute-start(f32[24,2,1,512]{3,2,1,0:T(1,128)S(1)} %get-tuple-element.70), channel_id=1, source_target_pairs={{0,8},{8,16},{16,24},{24,32},{32,40},{40,48},{48,56},{56,64},{64,7... | collective-permute-start | bytes 294920 | tf_op jit(solution)/shard_map/ppermute | solution.py:19
  41.4 26.0 %collective-permute-start.5 = (f32[24,2,1,512]{3,2,1,0:T(1,128)S(1)}, f32[24,2,1,512]{3,2,1,0:T(1,128)S(1)}, u32[]{:S(2)}, u32[]{:S(2)}) collective-permute-start(f32[24,2,1,512]{3,2,1,0:T(1,128)S(1)} %get-tuple-element.71), channel_id=1, source_target_pairs={{8,0},{16,8},{24,16},{32,24},{40,32},{48,40},{56,48},{64,56},{72,6... | collective-permute-start | bytes 294920 | tf_op jit(solution)/shard_map/ppermute | solution.py:21
  48.9 11.0 %collective-permute-start.6 = (f32[24,2,16,1]{3,2,1,0:T(8,128)S(1)}, f32[24,2,16,1]{3,2,1,0:T(8,128)S(1)}, u32[]{:S(2)}, u32[]{:S(2)}) collective-permute-start(f32[24,2,16,1]{3,2,1,0:T(8,128)S(1)} %get-tuple-element.72), channel_id=1, source_target_pairs={{0,1},{1,2},{2,3},{3,4},{4,5},{5,6},{6,7},{7,0},{8,9},{9,10},{10,1... | collective-permute-start | bytes 9224 | tf_op jit(solution)/shard_map/ppermute | solution.py:19
  49.8 15.3 %collective-permute-start.7 = (f32[24,2,16,1]{3,2,1,0:T(8,128)S(1)}, f32[24,2,16,1]{3,2,1,0:T(8,128)S(1)}, u32[]{:S(2)}, u32[]{:S(2)}) collective-permute-start(f32[24,2,16,1]{3,2,1,0:T(8,128)S(1)} %get-tuple-element.73), channel_id=1, source_target_pairs={{1,0},{2,1},{3,2},{4,3},{5,4},{6,5},{7,6},{0,7},{9,8},{10,9},{11,1... | collective-permute-start | bytes 9224 | tf_op jit(solution)/shard_map/ppermute | solution.py:21
where the time goes:
time: 71 us; the launch traced here: 70.8 us
  waiting for transfers between devices  31 us (44%)
  starting transfers between devices  17.4 us (25%)
  other arithmetic  12.6 us (18%)
  local copies, waits for them, and re-layouts  6.96 us (10%)
  matrix products  1.88 us (3%)
  between operations  0.88 us (1%)
    ppermute x4, waiting for transfers between devices, with_halo(): lax.ppermute(tail, axis, [(i, (i + 1) % count) for i in range(count)])  20 us
    ppermute x4, starting transfers between devices, with_halo(): lax.ppermute(head, axis, [((i + 1) % count, i) for i in range(count)])  14.3 us
    ppermute x4, waiting for transfers between devices, with_halo(): lax.ppermute(head, axis, [((i + 1) % count, i) for i in range(count)])  11.1 us
    ppermute x4, starting transfers between devices, with_halo(): lax.ppermute(tail, axis, [(i, (i + 1) % count) for i in range(count)])  3.12 us
    concatenate x4, other arithmetic, with_halo(): jnp.concatenate([lax.ppermute(tail, axis, [(i, (i + 1) % count) for i in...  2.21 us
    dot_general x1, matrix products, make_seeds(): jnp.einsum('pcv,clxy->pvlxy', probe_weights, onehot, precision=lax.Precis...  1.88 us
    unnamed x33, local copies, waits for them, and re-layouts  1.65 us
  transfers between devices with their start and end apart: 8, of which 5 were waited for; matrix products, arithmetic and copies ran while one was open for 7% of the time, Pallas kernels for 0%

commit v1 on v0

v1 whole, which is shorter than its diff:
```python
import functools

import jax
import jax.numpy as jnp
from jax import lax
from jax.experimental import pallas as pl
from jax.experimental.pallas import tpu as pltpu
from jax.sharding import PartitionSpec as P

MU = 0.2
KAPPA = 0.2 * 1.4 / (0.4 * 0.72)
BASE = 12
ROWS = 40


def pack_x(flow, colour, to_near, to_far):
    odd = lax.rem(lax.axis_index("gx"), 2)

    def fill(dst, start):
        for l in range(2):
            for v in range(5):
                dst[4 * v + 2 * l : 4 * v + 2 * l + 2, :] = flow[v, l, start : start + 2, :]
            dst[20 + 2 * l : 22 + 2 * l, :] = colour[l, start : start + 2, :].astype(jnp.float32)

    @pl.when(odd == 0)
    def _():
        fill(to_near, 14)
        fill(to_far, 0)

    @pl.when(odd == 1)
    def _():
        fill(to_near, 0)
        fill(to_far, 14)


def pack_y(flow, colour, from_near, from_far, ext, to_near, to_far):
    odd_x = lax.rem(lax.axis_index("gx"), 2)
    odd_y = lax.rem(lax.axis_index("gy"), 2)
    for l in range(2):
        for c in range(4):
            lanes = slice(128 * c, 128 * c + 128)
            for v in range(5):
                ext[v, l, c, BASE : BASE + 16, :] = flow[v, l, :, lanes]
            ext[5, l, c, BASE : BASE + 16, :] = colour[l, :, lanes].astype(jnp.float32)

    def halo(src, row):
        for l in range(2):
            for v in range(6):
                for c in range(4):
                    ext[v, l, c, row : row + 2, :] = src[4 * v + 2 * l : 4 * v + 2 * l + 2, 128 * c : 128 * c + 128]

    @pl.when(odd_x == 0)
    def _():
        halo(from_far, BASE - 2)
        halo(from_near, BASE + 16)

    @pl.when(odd_x == 1)
    def _():
        halo(from_near, BASE - 2)
        halo(from_far, BASE + 16)

    lane = lax.broadcasted_iota(jnp.int32, (24, 128), 1)

    def edge(c, first):
        made = jnp.zeros((24, 128), jnp.float32)
        for l in range(2):
            for v in range(6):
                at = 2 * (6 * l + v)
                cells = ext[v, l, c, BASE - 4 : BASE + 20, :]
                moved = pltpu.roll(cells, (at - first) % 128, 1)
                made = jnp.where((lane >= at) & (lane < at + 2), moved, made)
        return made

    left, right = edge(0, 0), edge(3, 126)

    @pl.when(odd_y == 0)
    def _():
        to_near[...] = right
        to_far[...] = left

    @pl.when(odd_y == 1)
    def _():
        to_near[...] = left
        to_far[...] = right


def tangent(ext, from_near, from_far, flags, table, out, rim, seeds, prim, speed, flux, stress, face):
    odd_y = lax.rem(lax.axis_index("gy"), 2)
    lane = lax.broadcasted_iota(jnp.int32, (24, 128), 1)

    def unpack(low, high):
        for l in range(2):
            for v in range(6):
                at = 2 * (6 * l + v)
                rim[v, l, BASE - 4 : BASE + 20, :] = jnp.where(
                    lane < 64,
                    pltpu.roll(high[...], (-at) % 128, 1),
                    pltpu.roll(low[...], (126 - at) % 128, 1),
                )

    @pl.when(odd_y == 0)
    def _():
        unpack(from_far, from_near)

    @pl.when(odd_y == 1)
    def _():
        unpack(from_near, from_far)

    def state(v, l, row, tiles=5):
        parts = [ext[v, l, c, row : row + 8, :] for c in range(4)]
        if tiles == 5:
            parts.append(rim[v, l, row : row + 8, :])
        return jnp.concatenate(parts, axis=1)

    def get(ref, f, l, row, tiles=5):
        return jnp.concatenate([ref[f, l, c, row : row + 8, :] for c in range(tiles)], axis=1)

    def put(ref, f, l, row, value):
        for c in range(value.shape[1] // 128):
            ref[f, l, c, row : row + 8, :] = value[:, 128 * c : 128 * c + 128]

    def ahead(value, step=1):
        return pltpu.roll(value, (-step) % value.shape[1], 1)

    for l in range(2):
        for row in (8, 16, 24):
            for c in range(5):
                if c < 4:
                    u5 = [ext[v, l, c, row : row + 8, :] for v in range(6)]
                else:
                    u5 = [rim[v, l, row : row + 8, :] for v in range(6)]
                shade = u5[5].astype(jnp.int32) & 127
                r = 1.0 / u5[0]
                vel = [u5[1 + e] * r for e in range(3)]
                half = 0.5 * (vel[0] * vel[0] + vel[1] * vel[1] + vel[2] * vel[2])
                pressure = 0.4 * (u5[4] - half * u5[0])
                heat = pressure * r
                total = u5[4] + pressure
                for e in range(3):
                    prim[e, l, c, row : row + 8, :] = vel[e]
                prim[3, l, c, row : row + 8, :] = heat
                inverse = []
                for e in range(3):
                    square = vel[e] * vel[e] + 1.4 * heat
                    inv = lax.rsqrt(square)
                    speed[3 * e, l, c, row : row + 8, :] = 0.25 * (square * inv)
                    inverse.append(0.25 * inv)
                for p in range(2):
                    d = []
                    for v in range(5):
                        row_of = jnp.broadcast_to(table[5 * p + v : 5 * p + v + 1, :], (8, 128))
                        d.append(jnp.take_along_axis(row_of, shade, axis=1, mode="promise_in_bounds"))
                        seeds[5 * p + v, l, c, row : row + 8, :] = d[v]
                    dvel = [(d[1 + e] - vel[e] * d[0]) * r for e in range(3)]
                    dpress = 0.4 * (d[4] - (vel[0] * d[1] + vel[1] * d[2] + vel[2] * d[3]) + half * d[0])
                    dheat = (dpress - heat * d[0]) * r
                    for e in range(3):
                        prim[4 + 4 * p + e, l, c, row : row + 8, :] = dvel[e]
                    prim[7 + 4 * p, l, c, row : row + 8, :] = dheat
                    warm = 0.7 * dheat
                    dtotal = d[4] + dpress
                    for e in range(3):
                        speed[3 * e + 1 + p, l, c, row : row + 8, :] = (vel[e] * dvel[e] + warm) * inverse[e]
                        for g in range(3):
                            move = d[1 + g] * vel[e] + u5[1 + g] * dvel[e]
                            if g == e:
                                move = move + dpress
                            flux[8 * e + 4 * p + g, l, c, row : row + 8, :] = move
                        flux[8 * e + 4 * p + 3, l, c, row : row + 8, :] = dtotal * vel[e] + total * dvel[e]

    quarter = 0.25 * MU
    for row in (8, 16, 24):
        for k in range(3):
            grad_z = [2.0 * (get(prim, 4 * k + q, 1, row) - get(prim, 4 * k + q, 0, row)) for q in range(4)]
            for l in range(2):
                here = [get(prim, 4 * k + q, l, row) for q in range(4)]
                grad_x = [get(prim, 4 * k + q, l, row + 1) - get(prim, 4 * k + q, l, row - 1) for q in range(4)]
                grad_y = [ahead(h, 1) - ahead(h, -1) for h in here]
                third = (2.0 / 3.0) * (grad_x[0] + grad_y[1] + grad_z[2])
                base = 0 if k == 0 else 6 + 9 * (k - 1)
                put(stress, base, l, row, quarter * (2.0 * grad_x[0] - third))
                put(stress, base + 1, l, row, quarter * (grad_y[0] + grad_x[1]))
                put(stress, base + 2, l, row, quarter * (grad_z[0] + grad_x[2]))
                put(stress, base + 3, l, row, quarter * (2.0 * grad_y[1] - third))
                put(stress, base + 4, l, row, quarter * (grad_z[1] + grad_y[2]))
                put(stress, base + 5, l, row, quarter * (2.0 * grad_z[2] - third))
                if k > 0:
                    put(stress, base + 6, l, row, (0.25 * KAPPA) * grad_x[3])
                    put(stress, base + 7, l, row, (0.25 * KAPPA) * grad_y[3])
                    put(stress, base + 8, l, row, (0.25 * KAPPA) * grad_z[3])

    parts_of = ((0, 1, 2), (1, 3, 4), (2, 4, 5))

    for l in range(2):
        for row in (8, 16, 24):
            jump = [state(v, l, row + 1, 4) - state(v, l, row, 4) for v in range(5)]
            s_sum = get(speed, 0, l, row, 4) + get(speed, 0, l, row + 1, 4)
            v_sum = [0.5 * (get(prim, e, l, row, 4) + get(prim, e, l, row + 1, 4)) for e in range(3)]
            t_sum = [get(stress, t, l, row, 4) + get(stress, t, l, row + 1, 4) for t in parts_of[0]]
            for p in range(2):
                ds = get(speed, 1 + p, l, row, 4) + get(speed, 1 + p, l, row + 1, 4)
                for v in range(5):
                    djump = get(seeds, 5 * p + v, l, row + 1, 4) - get(seeds, 5 * p + v, l, row, 4)
                    made = ds * jump[v] + s_sum * djump
                    if v == 4:
                        for e in range(3):
                            f = 6 + 9 * p + parts_of[0][e]
                            dt = get(stress, f, l, row, 4) + get(stress, f, l, row + 1, 4)
                            dv = 0.5 * (get(prim, 4 + 4 * p + e, l, row, 4) + get(prim, 4 + 4 * p + e, l, row + 1, 4))
                            made = made + v_sum[e] * dt + dv * t_sum[e]
                    put(face, 5 * p + v, l, row, made)

    for t in range(2):
        row = BASE + 8 * t
        solid = flags[8 * t : 8 * t + 8, :] == 1
        jump_z = [state(v, 1, row, 4) - state(v, 0, row, 4) for v in range(5)]
        s_z = get(speed, 6, 0, row, 4) + get(speed, 6, 1, row, 4)
        v_z = [0.5 * (get(prim, e, 0, row, 4) + get(prim, e, 1, row, 4)) for e in range(3)]
        t_z = [get(stress, i, 0, row, 4) + get(stress, i, 1, row, 4) for i in parts_of[2]]
        through = []
        for p in range(2):
            ds = get(speed, 7 + p, 0, row, 4) + get(speed, 7 + p, 1, row, 4)
            for v in range(5):
                seed0, seed1 = get(seeds, 5 * p + v, 0, row, 4), get(seeds, 5 * p + v, 1, row, 4)
                if v == 0:
                    mean = get(seeds, 5 * p + 3, 0, row, 4) + get(seeds, 5 * p + 3, 1, row, 4)
                else:
                    f = 16 + 4 * p + v - 1
                    mean = get(flux, f, 0, row, 4) + get(flux, f, 1, row, 4)
                made = 0.5 * mean - (ds * jump_z[v] + s_z * (seed1 - seed0))
                if 1 <= v <= 3:
                    f = 6 + 9 * p + parts_of[2][v - 1]
                    made = made - (get(stress, f, 0, row, 4) + get(stress, f, 1, row, 4))
                if v == 4:
                    work = get(stress, 6 + 9 * p + 8, 0, row, 4) + get(stress, 6 + 9 * p + 8, 1, row, 4)
                    for e in range(3):
                        f = 6 + 9 * p + parts_of[2][e]
                        dt = get(stress, f, 0, row, 4) + get(stress, f, 1, row, 4)
                        dv = 0.5 * (get(prim, 4 + 4 * p + e, 0, row, 4) + get(prim, 4 + 4 * p + e, 1, row, 4))
                        work = work + v_z[e] * dt + dv * t_z[e]
                    made = made - work
                through.append(made)
        for l in range(2):
            jump, v_sum, t_sum = [], [], []
            for v in range(5):
                here = state(v, l, row)
                jump.append(ahead(here) - here)
            for e in range(3):
                here = get(prim, e, l, row)
                v_sum.append(0.5 * (here + ahead(here)))
                here = get(stress, parts_of[1][e], l, row)
                t_sum.append(here + ahead(here))
            here = get(speed, 3, l, row)
            s_sum = here + ahead(here)
            for p in range(2):
                here = get(speed, 4 + p, l, row)
                ds = here + ahead(here)
                for v in range(5):
                    here = get(seeds, 5 * p + v, l, row)
                    made = ds * jump[v] + s_sum * (ahead(here) - here)
                    if v == 4:
                        for e in range(3):
                            here = get(stress, 6 + 9 * p + parts_of[1][e], l, row)
                            dt = here + ahead(here)
                            here = get(prim, 4 + 4 * p + e, l, row)
                            dv = 0.5 * (here + ahead(here))
                            made = made + v_sum[e] * dt + dv * t_sum[e]
                    if v == 0:
                        cell = get(seeds, 5 * p + 2, l, row)
                    else:
                        cell = get(flux, 8 + 4 * p + v - 1, l, row)
                    third = (1.0 / 12.0) * cell
                    cell = (8.0 / 12.0) * cell - ahead(third, 1) - ahead(third, -1)
                    if v > 0:
                        f = 7 if v == 4 else parts_of[1][v - 1]
                        cell = cell - get(stress, 6 + 9 * p + f, l, row)
                    made = made - cell - ahead(cell)
                    total = (made - ahead(made, -1))[:, :512]
                    if v == 0:
                        at = lambda s: get(seeds, 5 * p + 1, l, row + s, 4)
                    else:
                        at = lambda s: get(flux, 4 * p + v - 1, l, row + s, 4)
                    total = total - (8.0 / 12.0) * (at(1) - at(-1)) + (1.0 / 12.0) * (at(2) - at(-2))
                    if v > 0:
                        f = 6 + 9 * p + (6 if v == 4 else parts_of[0][v - 1])
                        total = total + get(stress, f, l, row + 1, 4) - get(stress, f, l, row - 1, 4)
                    total = total + get(face, 5 * p + v, l, row, 4) - get(face, 5 * p + v, l, row - 1, 4)
                    wall = through[5 * p + v]
                    total = total - wall if l == 0 else total + wall
                    seed = get(seeds, 5 * p + v, l, row, 4)
                    out[p, v, l, 8 * t : 8 * t + 8, :] = jnp.where(solid, -seed, total)


def swap(value, axis, offset):
    count = lax.axis_size(axis)
    pairs = []
    for k in range(0, count, 2):
        i, j = (k + offset) % count, (k + offset + 1) % count
        pairs += [(i, j), (j, i)]
    return lax.ppermute(value, axis, pairs)


def local(flow_state, colour_map, cell_flags, probe_weights):
    f32 = jnp.float32
    vmem = pl.BlockSpec(memory_space=pltpu.VMEM)
    params = pltpu.CompilerParams(vmem_limit_bytes=48 * 1024 * 1024)

    def call(kernel, shapes, n_in, scratch=()):
        return pl.pallas_call(
            kernel,
            out_shape=[jax.ShapeDtypeStruct(s, f32) for s in shapes],
            in_specs=[vmem] * n_in,
            out_specs=[vmem] * len(shapes),
            scratch_shapes=[pltpu.VMEM(s, f32) for s in scratch],
            compiler_params=params,
        )

    table = jnp.pad(jnp.transpose(probe_weights, (0, 2, 1)).reshape(10, 27), ((0, 6), (0, 101)))
    x_near, x_far = call(pack_x, [(24, 512)] * 2, 2)(flow_state, colour_map)
    x_far = swap(x_far, "gx", 1)
    x_near = swap(x_near, "gx", 0)
    ext, y_near, y_far = call(pack_y, [(6, 2, 4, ROWS, 128), (24, 128), (24, 128)], 4)(
        flow_state, colour_map, x_near, x_far
    )
    y_far = swap(y_far, "gy", 1)
    y_near = swap(y_near, "gy", 0)
    fields = lambda n: (n, 2, 5, ROWS, 128)
    (out,) = call(
        tangent,
        [(2, 5, 2, 16, 512)],
        5,
        [(6, 2, ROWS, 128), fields(10), fields(12), fields(9), fields(24), fields(24), (10, 2, 4, ROWS, 128)],
    )(ext, y_near, y_far, cell_flags, table)
    return out


def solution(mesh):
    return jax.shard_map(
        local,
        mesh=mesh,
        in_specs=(P(None, None, "gx", "gy"), P(None, "gx", "gy"), P("gx", "gy"), P()),
        out_specs=P(None, None, None, "gx", "gy"),
        check_vma=False,
    )
```

time: 71 us -> 27.8 us (0.39)
  the two profiles are of different devices: /device:TPU:32 before, /device:TPU:56 now
where the time goes in v1:
time: 27.8 us; the launch traced here: 27.6 us
  starting transfers between devices  9.56 us (34%)
  Pallas kernels  9.24 us (33%)
  waiting for transfers between devices  6.96 us (25%)
  local copies, waits for them, and re-layouts  1.84 us (7%)
    ppermute x4, starting transfers between devices, swap(): return lax.ppermute(value, axis, pairs)  9.56 us
    pallas_call x1, Pallas kernels, local(): call(tangent, [(2, 5, 2, 16, 512)], 5, [(6, 2, ROWS, 128), fields(10), fi...  9 us
    ppermute x4, waiting for transfers between devices, swap(): return lax.ppermute(value, axis, pairs)  6.96 us
    unnamed x8, local copies, waits for them, and re-layouts  1.82 us
  transfers between devices with their start and end apart: 4, of which 3 were waited for; matrix products, arithmetic and copies ran while one was open for 0% of the time, Pallas kernels for 0%

profile of v1, /device:TPU:56, one launch (start us, length us, event | category | flops | bytes accessed | tf_op | source)
XLA Modules:
  0.0 27.6 jit_solution(10306235293936601097)
XLA Ops:
  0.0 0.0 copy-start
  0.0 1.0 %copy-done = f32[5,2,16,512]{3,2,1,0:T(8,128)S(1)} copy-done((f32[5,2,16,512]{3,2,1,0:T(8,128)S(1)}, f32[5,2,16,512]{3,2,1,0:T(8,128)}, u32[]{:S(2)}) %copy-start) | copy-done | bytes 327704
  1.0 0.0 copy-start.1
  1.0 0.8 %copy-done.1 = s32[2,16,512]{2,1,0:T(8,128)S(1)} copy-done((s32[2,16,512]{2,1,0:T(8,128)S(1)}, s32[2,16,512]{2,1,0:T(8,128)}, u32[]{:S(2)}) %copy-start.1) | copy-done | bytes 65560
  1.9 0.1 collective-permute-start
  2.0 7.7 %collective-permute-start.1 = (f32[24,512]{1,0:T(8,128)S(1)}, f32[24,512]{1,0:T(8,128)S(1)}, u32[]{:S(2)}, u32[]{:S(2)}) collective-permute-start(f32[24,512]{1,0:T(8,128)S(1)} %get-tuple-element.11), channel_id=1, source_target_pairs={{8,16},{16,8},{24,32},{32,24},{40,48},{48,40},{56,64},{64,56},{72,... | collective-permute-start | bytes 147464 | tf_op jit(solution)/shard_map/ppermute | solution.py:300
  9.7 0.0 collective-permute-done.from_near
  9.7 1.8 %collective-permute-done.1.from_far = f32[24,512]{1,0:T(8,128)S(1)} collective-permute-done((f32[24,512]{1,0:T(8,128)S(1)}, f32[24,512]{1,0:T(8,128)S(1)}, u32[]{:S(2)}, u32[]{:S(2)}) %collective-permute-start.1) | collective-permute-done | bytes 49184 | tf_op jit(solution)/shard_map/ppermute | solution.py:300
  11.4 0.0 copy-start.3
  11.4 0.2 shard_map.47
  11.7 0.0 copy-start.2
  11.7 1.2 %collective-permute-start.2 = (f32[24,128]{1,0:T(8,128)S(1)}, f32[24,128]{1,0:T(8,128)S(1)}, u32[]{:S(2)}, u32[]{:S(2)}) collective-permute-start(f32[24,128]{1,0:T(8,128)S(1)} %get-tuple-element.13), channel_id=1, source_target_pairs={{0,1},{1,0},{2,3},{3,2},{4,5},{5,4},{6,7},{7,6},{8,9},{9,8},{10,11... | collective-permute-start | bytes 36872 | tf_op jit(solution)/shard_map/ppermute | solution.py:300
  12.8 0.6 %collective-permute-start.3 = (f32[24,128]{1,0:T(8,128)S(1)}, f32[24,128]{1,0:T(8,128)S(1)}, u32[]{:S(2)}, u32[]{:S(2)}) collective-permute-start(f32[24,128]{1,0:T(8,128)S(1)} %get-tuple-element.14), channel_id=1, source_target_pairs={{1,2},{2,1},{3,4},{4,3},{5,6},{6,5},{7,0},{0,7},{9,10},{10,9},{11,... | collective-permute-start | bytes 36872 | tf_op jit(solution)/shard_map/ppermute | solution.py:300
  13.4 0.0 copy-done.3
  13.5 2.0 %collective-permute-done.2.from_near = f32[24,128]{1,0:T(8,128)S(1)} collective-permute-done((f32[24,128]{1,0:T(8,128)S(1)}, f32[24,128]{1,0:T(8,128)S(1)}, u32[]{:S(2)}, u32[]{:S(2)}) %collective-permute-start.2) | collective-permute-done | bytes 12320 | tf_op jit(solution)/shard_map/ppermute | solution.py:300
  15.5 3.2 %collective-permute-done.3.from_far = f32[24,128]{1,0:T(8,128)S(1)} collective-permute-done((f32[24,128]{1,0:T(8,128)S(1)}, f32[24,128]{1,0:T(8,128)S(1)}, u32[]{:S(2)}, u32[]{:S(2)}) %collective-permute-start.3) | collective-permute-done | bytes 12320 | tf_op jit(solution)/shard_map/ppermute | solution.py:300
  18.6 0.0 copy-done.2
  18.6 9.0 %shard_map.48 = f32[2,5,2,16,512]{4,3,2,1,0:T(8,128)} custom-call(f32[6,2,4,40,128]{4,3,2,1,0:T(8,128)S(1)} %get-tuple-element.12.ext, f32[24,128]{1,0:T(8,128)S(1)} %collective-permute-done.2.from_near, f32[24,128]{1,0:T(8,128)S(1)} %collective-permute-done.3.from_far, s32[16,512]{1,0:T(8,128)S(1)} %copy-done.2, f32[16,128]{1,0:T(8,128)S(1)} %pad.4.table), custom_call_target="tpu_custom_call" | custom-call | tf_op jit(solution)/shard_map/pallas_call | solution.py:328
  (4 shorter events, 0.1 us)
Async XLA Ops:
  0.0 1.0 %copy-start = (f32[5,2,16,512]{3,2,1,0:T(8,128)S(1)}, f32[5,2,16,512]{3,2,1,0:T(8,128)}, u32[]{:S(2)}) copy-start(f32[5,2,16,512]{3,2,1,0:T(8,128)} %flow.3) | copy-start | bytes 983044
  1.0 0.8 %copy-start.1 = (s32[2,16,512]{2,1,0:T(8,128)S(1)}, s32[2,16,512]{2,1,0:T(8,128)}, u32[]{:S(2)}) copy-start(s32[2,16,512]{2,1,0:T(8,128)} %colour.3) | copy-start | bytes 196612
  1.9 7.8 %collective-permute-start = (f32[24,512]{1,0:T(8,128)S(1)}, f32[24,512]{1,0:T(8,128)S(1)}, u32[]{:S(2)}, u32[]{:S(2)}) collective-permute-start(f32[24,512]{1,0:T(8,128)S(1)} %get-tuple-element.10), channel_id=1, source_target_pairs={{0,8},{8,0},{16,24},{24,16},{32,40},{40,32},{48,56},{56,48},{64,72... | collective-permute-start | bytes 147464 | tf_op jit(solution)/shard_map/ppermute | solution.py:300
  2.0 9.5 %collective-permute-start.1 = (f32[24,512]{1,0:T(8,128)S(1)}, f32[24,512]{1,0:T(8,128)S(1)}, u32[]{:S(2)}, u32[]{:S(2)}) collective-permute-start(f32[24,512]{1,0:T(8,128)S(1)} %get-tuple-element.11), channel_id=1, source_target_pairs={{8,16},{16,8},{24,32},{32,24},{40,48},{48,40},{56,64},{64,56},{72,... | collective-permute-start | bytes 147464 | tf_op jit(solution)/shard_map/ppermute | solution.py:300
  11.4 2.0 %copy-start.3 = (f32[2,27,5]{1,0,2:T(2,128)S(1)}, f32[2,27,5]{1,0,2:T(2,128)}, u32[]{:S(2)}) copy-start(f32[2,27,5]{1,0,2:T(2,128)} %param.7) | copy-start | bytes 3244
  11.7 7.0 %copy-start.2 = (s32[16,512]{1,0:T(8,128)S(1)}, s32[16,512]{1,0:T(8,128)}, u32[]{:S(2)}) copy-start(s32[16,512]{1,0:T(8,128)} %flags.1) | copy-start | bytes 98308
  11.7 3.8 %collective-permute-start.2 = (f32[24,128]{1,0:T(8,128)S(1)}, f32[24,128]{1,0:T(8,128)S(1)}, u32[]{:S(2)}, u32[]{:S(2)}) collective-permute-start(f32[24,128]{1,0:T(8,128)S(1)} %get-tuple-element.13), channel_id=1, source_target_pairs={{0,1},{1,0},{2,3},{3,2},{4,5},{5,4},{6,7},{7,6},{8,9},{9,8},{10,11... | collective-permute-start | bytes 36872 | tf_op jit(solution)/shard_map/ppermute | solution.py:300
  12.8 5.8 %collective-permute-start.3 = (f32[24,128]{1,0:T(8,128)S(1)}, f32[24,128]{1,0:T(8,128)S(1)}, u32[]{:S(2)}, u32[]{:S(2)}) collective-permute-start(f32[24,128]{1,0:T(8,128)S(1)} %get-tuple-element.14), channel_id=1, source_target_pairs={{1,2},{2,1},{3,4},{4,3},{5,6},{6,5},{7,0},{0,7},{9,10},{10,9},{11,... | collective-permute-start | bytes 36872 | tf_op jit(solution)/shard_map/ppermute | solution.py:300

commit v2 on v1

v2 whole, which is shorter than its diff:
```python
import jax
import jax.numpy as jnp
from jax import lax
from jax.experimental import pallas as pl
from jax.experimental.pallas import tpu as pltpu
from jax.sharding import PartitionSpec as P

MU = 0.2
KAPPA = 0.2 * 1.4 / (0.4 * 0.72)
BASE = 12
ROWS = 40
STATE, SEED, PRIM, SPEED, FLUX, FIELDS = 0, 6, 16, 28, 31, 39
TENSOR = ((0, 1, 2), (1, 3, 4), (2, 4, 5))


def get(ref, f, l, row):
    tiles = [ref[f, l, c, row : row + 8, :] for c in range(ref.shape[2])]
    return tiles[0] if len(tiles) == 1 else jnp.concatenate(tiles, axis=1)


def put(ref, f, l, row, value):
    for c in range(ref.shape[2]):
        ref[f, l, c, row : row + 8, :] = value[:, 128 * c : 128 * c + 128]


def ahead(value, step=1):
    return pltpu.roll(value, (-step) % value.shape[1], 1)


def pointwise(bank, table, rows, speed_yz=None, flux_yz=None):
    for l in range(2):
        for row in rows:
            for c in range(bank.shape[2]):
                at = (l, c, slice(row, row + 8), slice(None))
                u = [bank[(STATE + v,) + at] for v in range(5)]
                shade = bank[(STATE + 5,) + at].astype(jnp.int32) & 127
                r = 1.0 / u[0]
                vel = [u[1 + e] * r for e in range(3)]
                half = 0.5 * (vel[0] * vel[0] + vel[1] * vel[1] + vel[2] * vel[2])
                pressure = 0.4 * (u[4] - half * u[0])
                heat = pressure * r
                total = u[4] + pressure
                for e in range(3):
                    bank[(PRIM + e,) + at] = vel[e]
                bank[(PRIM + 3,) + at] = heat
                axes = range(1 if flux_yz is None else 3)
                inverse = []
                for e in axes:
                    square = vel[e] * vel[e] + 1.4 * heat
                    inv = lax.rsqrt(square)
                    if e == 0:
                        bank[(SPEED,) + at] = 0.25 * (square * inv)
                    else:
                        speed_yz[(3 * e - 3,) + at] = 0.25 * (square * inv)
                    inverse.append(0.25 * inv)
                for p in range(2):
                    d = []
                    for v in range(5):
                        line = jnp.broadcast_to(table[5 * p + v : 5 * p + v + 1, :], (8, 128))
                        d.append(jnp.take_along_axis(line, shade, axis=1, mode="promise_in_bounds"))
                        bank[(SEED + 5 * p + v,) + at] = d[v]
                    dvel = [(d[1 + e] - vel[e] * d[0]) * r for e in range(3)]
                    dpress = 0.4 * (d[4] - (vel[0] * d[1] + vel[1] * d[2] + vel[2] * d[3]) + half * d[0])
                    dheat = (dpress - heat * d[0]) * r
                    for e in range(3):
                        bank[(PRIM + 4 + 4 * p + e,) + at] = dvel[e]
                    bank[(PRIM + 7 + 4 * p,) + at] = dheat
                    warm = 0.7 * dheat
                    dtotal = d[4] + dpress
                    for e in axes:
                        dspeed = (vel[e] * dvel[e] + warm) * inverse[e]
                        fluxes = []
                        for g in range(3):
                            move = d[1 + g] * vel[e] + u[1 + g] * dvel[e]
                            fluxes.append(move + dpress if g == e else move)
                        fluxes.append(dtotal * vel[e] + total * dvel[e])
                        if e == 0:
                            bank[(SPEED + 1 + p,) + at] = dspeed
                        else:
                            speed_yz[(3 * e - 2 + p,) + at] = dspeed
                        for g in range(4):
                            if e == 0:
                                bank[(FLUX + 4 * p + g,) + at] = fluxes[g]
                            else:
                                flux_yz[(8 * e - 8 + 4 * p + g,) + at] = fluxes[g]


def inviscid_yz(bank, speed_yz, flux_yz, cell, face, acc):
    places = [(l, t) for l in range(2) for t in range(2)]
    for l, t in places:
        row = BASE + 8 * t
        for p in range(2):
            for v in range(5):
                if v == 0:
                    f = get(bank, SEED + 5 * p + 2, l, row)
                else:
                    f = get(flux_yz, 4 * p + v - 1, l, row)
                put(cell, 5 * p + v, l, 8 * t, (8.0 / 12.0) * f - (1.0 / 12.0) * (ahead(f) + ahead(f, -1)))
    for l, t in places:
        row = BASE + 8 * t
        here = get(speed_yz, 0, l, row)
        s_sum = here + ahead(here)
        ds = []
        for p in range(2):
            here = get(speed_yz, 1 + p, l, row)
            ds.append(here + ahead(here))
        for v in range(5):
            here = get(bank, STATE + v, l, row)
            jump = ahead(here) - here
            for p in range(2):
                here = get(bank, SEED + 5 * p + v, l, row)
                central = get(cell, 5 * p + v, l, 8 * t)
                made = ds[p] * jump + s_sum * (ahead(here) - here) - (central + ahead(central))
                put(face, 5 * p + v, l, 8 * t, made)
    for t in range(2):
        row = BASE + 8 * t
        s_sum = get(speed_yz, 3, 0, row) + get(speed_yz, 3, 1, row)
        ds = [get(speed_yz, 4 + p, 0, row) + get(speed_yz, 4 + p, 1, row) for p in range(2)]
        for v in range(5):
            jump = get(bank, STATE + v, 1, row) - get(bank, STATE + v, 0, row)
            for p in range(2):
                if v == 0:
                    mean = get(bank, SEED + 5 * p + 3, 0, row) + get(bank, SEED + 5 * p + 3, 1, row)
                else:
                    mean = get(flux_yz, 8 + 4 * p + v - 1, 0, row) + get(flux_yz, 8 + 4 * p + v - 1, 1, row)
                djump = get(bank, SEED + 5 * p + v, 1, row) - get(bank, SEED + 5 * p + v, 0, row)
                wall = 0.5 * mean - (ds[p] * jump + s_sum * djump)
                for l in range(2):
                    made = get(face, 5 * p + v, l, 8 * t)
                    made = made - ahead(made, -1)
                    put(acc, 5 * p + v, l, 8 * t, made + wall if l == 1 else made - wall)


def stresses(bank, stress, rows):
    quarter = 0.25 * MU
    for row in rows:
        for k in range(3):
            q = PRIM + 4 * k
            grad_z = [2.0 * (get(bank, q + i, 1, row) - get(bank, q + i, 0, row)) for i in range(4 if k else 3)]
            for l in range(2):
                count = range(4 if k else 3)
                grad_x = [get(bank, q + i, l, row + 1) - get(bank, q + i, l, row - 1) for i in count]
                here = [get(bank, q + i, l, row) for i in count]
                grad_y = [ahead(h, 1) - ahead(h, -1) for h in here]
                third = (2.0 / 3.0) * (grad_x[0] + grad_y[1] + grad_z[2])
                base = 9 * k - 3 if k else 0
                put(stress, base, l, row, quarter * (2.0 * grad_x[0] - third))
                put(stress, base + 1, l, row, quarter * (grad_y[0] + grad_x[1]))
                put(stress, base + 2, l, row, quarter * (grad_z[0] + grad_x[2]))
                put(stress, base + 3, l, row, quarter * (2.0 * grad_y[1] - third))
                put(stress, base + 4, l, row, quarter * (grad_z[1] + grad_y[2]))
                put(stress, base + 5, l, row, quarter * (2.0 * grad_z[2] - third))
                if k > 0:
                    put(stress, base + 6, l, row, (0.25 * KAPPA) * grad_x[3])
                    put(stress, base + 7, l, row, (0.25 * KAPPA) * grad_y[3])
                    put(stress, base + 8, l, row, (0.25 * KAPPA) * grad_z[3])


def x_faces(bank, stress, xface, rows):
    for l in range(2):
        for row in rows:
            pair = lambda ref, f: get(ref, f, l, row) + get(ref, f, l, row + 1)
            s_sum = pair(bank, SPEED)
            ds = [pair(bank, SPEED + 1 + p) for p in range(2)]
            for v in range(5):
                jump = get(bank, STATE + v, l, row + 1) - get(bank, STATE + v, l, row)
                for p in range(2):
                    f = SEED + 5 * p + v
                    made = ds[p] * jump + s_sum * (get(bank, f, l, row + 1) - get(bank, f, l, row))
                    if v == 4:
                        work = 0.0
                        for e in range(3):
                            i = TENSOR[0][e]
                            work = work + pair(bank, PRIM + e) * pair(stress, 6 + 9 * p + i)
                            work = work + pair(bank, PRIM + 4 + 4 * p + e) * pair(stress, i)
                        made = made + 0.5 * work
                    put(xface, 5 * p + v, l, row, made)


def finish(bank, stress, xface, yface, zface, acc, flags, out):
    for t in range(2):
        row = BASE + 8 * t
        for l in range(2):
            def pair(ref, f):
                here = get(ref, f, l, row)
                return here + ahead(here)

            v_sum = [pair(bank, PRIM + e) for e in range(3)]
            t_sum = [pair(stress, i) for i in TENSOR[1]]
            for p in range(2):
                work = 0.0
                for e in range(3):
                    work = work + v_sum[e] * pair(stress, 6 + 9 * p + TENSOR[1][e])
                    work = work + pair(bank, PRIM + 4 + 4 * p + e) * t_sum[e]
                put(yface, p, l, 8 * t, 0.5 * work)
        both = lambda ref, f: get(ref, f, 0, row) + get(ref, f, 1, row)
        v_sum = [both(bank, PRIM + e) for e in range(3)]
        t_sum = [both(stress, i) for i in TENSOR[2]]
        for p in range(2):
            work = 0.0
            for e in range(3):
                dt = both(stress, 6 + 9 * p + TENSOR[2][e])
                put(zface, 4 * p + e, 0, 8 * t, dt)
                work = work + v_sum[e] * dt + both(bank, PRIM + 4 + 4 * p + e) * t_sum[e]
            put(zface, 4 * p + 3, 0, 8 * t, 0.5 * work + both(stress, 6 + 9 * p + 8))
    for t in range(2):
        row = BASE + 8 * t
        solid = flags(8 * t) == 1
        for l in range(2):
            for p in range(2):
                for v in range(5):
                    f = SEED + 5 * p + 1 if v == 0 else FLUX + 4 * p + v - 1
                    total = get(acc, 5 * p + v, l, 8 * t)
                    total = total - (8.0 / 12.0) * (get(bank, f, l, row + 1) - get(bank, f, l, row - 1))
                    total = total + (1.0 / 12.0) * (get(bank, f, l, row + 2) - get(bank, f, l, row - 2))
                    total = total + get(xface, 5 * p + v, l, row) - get(xface, 5 * p + v, l, row - 1)
                    if v > 0:
                        f = 6 + 9 * p + (6 if v == 4 else TENSOR[0][v - 1])
                        total = total + get(stress, f, l, row + 1) - get(stress, f, l, row - 1)
                        here = get(stress, 6 + 9 * p + (7 if v == 4 else TENSOR[1][v - 1]), l, row)
                        if v == 4:
                            work = get(yface, p, l, 8 * t)
                            total = total + ahead(here) + work - ahead(here + work, -1)
                        else:
                            total = total + ahead(here) - ahead(here, -1)
                        wall = get(zface, 4 * p + v - 1, 0, 8 * t)
                        total = total + wall if l == 0 else total - wall
                    put(out, 5 * p + v, l, 8 * t, jnp.where(solid, -get(bank, SEED + 5 * p + v, l, row), total))


def pack_x(flow, colour, flags, weights, to_near, to_far, flow_out, colour_out, flags_out, weights_out, sems):
    pairs = ((flow, flow_out), (colour, colour_out), (flags, flags_out), (weights, weights_out))
    copies = [pltpu.make_async_copy(src, dst, sems.at[i]) for i, (src, dst) in enumerate(pairs)]
    for copy in copies:
        copy.start()
    for copy in copies:
        copy.wait()
    odd = lax.rem(lax.axis_index("gx"), 2)

    def fill(dst, start):
        for l in range(2):
            for v in range(5):
                dst[4 * v + 2 * l : 4 * v + 2 * l + 2, :] = flow_out[v, l, start : start + 2, :]
            dst[20 + 2 * l : 22 + 2 * l, :] = colour_out[l, start : start + 2, :].astype(jnp.float32)

    @pl.when(odd == 0)
    def _():
        fill(to_near, 14)
        fill(to_far, 0)

    @pl.when(odd == 1)
    def _():
        fill(to_near, 0)
        fill(to_far, 14)


def own_cells(flow, colour, weights, bank, acc, table, speed_yz, flux_yz, cell, face):
    for p in range(2):
        for v in range(5):
            line = weights[v, p : p + 1, :]
            table[5 * p + v : 5 * p + v + 1, :] = jnp.concatenate([line, jnp.zeros((1, 101), jnp.float32)], axis=1)
    for l in range(2):
        for c in range(4):
            lanes = slice(128 * c, 128 * c + 128)
            for v in range(5):
                bank[STATE + v, l, c, BASE : BASE + 16, :] = flow[v, l, :, lanes]
            bank[STATE + 5, l, c, BASE : BASE + 16, :] = colour[l, :, lanes].astype(jnp.float32)
    pointwise(bank, table, (BASE, BASE + 8), speed_yz, flux_yz)
    inviscid_yz(bank, speed_yz, flux_yz, cell, face, acc)


def x_halo(near, far, store):
    odd = lax.rem(lax.axis_index("gx"), 2)

    def fill(src, row):
        for l in range(2):
            for v in range(6):
                store(v, l, row, src, 4 * v + 2 * l)

    @pl.when(odd == 0)
    def _():
        fill(far, BASE - 2)
        fill(near, BASE + 16)

    @pl.when(odd == 1)
    def _():
        fill(near, BASE - 2)
        fill(far, BASE + 16)


def pack_y(flow, colour, near, far, table, edge, to_near, to_far):
    for l in range(2):
        for side in range(2):
            lanes = slice(384 * side, 384 * side + 128)
            for v in range(5):
                edge[v, l, side, BASE : BASE + 16, :] = flow[v, l, :, lanes]
            edge[5, l, side, BASE : BASE + 16, :] = colour[l, :, lanes].astype(jnp.float32)

    def store(v, l, row, src, at):
        for side in range(2):
            edge[v, l, side, row : row + 2, :] = src[at : at + 2, 384 * side : 384 * side + 128]

    x_halo(near, far, store)
    lane = lax.broadcasted_iota(jnp.int32, (24, 128), 1)

    def columns(side, first):
        made = jnp.zeros((24, 128), jnp.float32)
        for l in range(2):
            for v in range(6):
                at = 2 * (6 * l + v)
                moved = pltpu.roll(edge[v, l, side, BASE - 4 : BASE + 20, :], (at - first) % 128, 1)
                made = jnp.where((lane >= at) & (lane < at + 2), moved, made)
        return made

    left, right = columns(0, 0), columns(1, 126)
    odd = lax.rem(lax.axis_index("gy"), 2)

    @pl.when(odd == 0)
    def _():
        to_near[...] = right
        to_far[...] = left

    @pl.when(odd == 1)
    def _():
        to_near[...] = left
        to_far[...] = right


def whole_rows(near, far, table, flags, bank_in, acc, bank, result, out, stress, xface, yface, zface, sem):
    def store(v, l, row, src, at):
        for c in range(4):
            bank[STATE + v, l, c, row : row + 2, :] = src[at : at + 2, 128 * c : 128 * c + 128]

    x_halo(near, far, store)
    pointwise(bank, table, (BASE - 4, BASE + 12))
    rows = (BASE - 4, BASE + 4, BASE + 12)
    stresses(bank, stress, rows)
    x_faces(bank, stress, xface, rows)
    finish(bank, stress, xface, yface, zface, acc, lambda row: flags[row : row + 8, :], result)
    copies = []
    for c in (1, 2):
        copies.append(
            pltpu.make_async_copy(result.at[:, :, c], out.at[:, :, :, 128 * c : 128 * c + 128], sem.at[c - 1])
        )
        copies[-1].start()
    for copy in copies:
        copy.wait()


def edge_columns(
    near, far, edge, table, flags, result, out_in, out, bank, acc, speed_yz, flux_yz, cell, face, stress, xface, yface,
    zface, final, staged, sem,
):
    lane = lax.broadcasted_iota(jnp.int32, (24, 128), 1)
    odd = lax.rem(lax.axis_index("gy"), 2)

    def unpack(low, high):
        for l in range(2):
            for v in range(6):
                at = 2 * (6 * l + v)
                first = edge[v, l, 0, BASE - 4 : BASE + 20, :]
                last = pltpu.roll(edge[v, l, 1, BASE - 4 : BASE + 20, :], 64, 1)
                below = pltpu.roll(low[...], (126 - at) % 128, 1)
                above = pltpu.roll(high[...], 64 - at, 1)
                made = jnp.where(lane < 32, first, last)
                made = jnp.where(lane >= 64, above, made)
                bank[STATE + v, l, 0, BASE - 4 : BASE + 20, :] = jnp.where(lane >= 96, below, made)

    @pl.when(odd == 0)
    def _():
        unpack(far, near)

    @pl.when(odd == 1)
    def _():
        unpack(near, far)

    rows = (BASE - 4, BASE + 4, BASE + 12)
    pointwise(bank, table, rows, speed_yz, flux_yz)
    inviscid_yz(bank, speed_yz, flux_yz, cell, face, acc)
    stresses(bank, stress, rows)
    x_faces(bank, stress, xface, rows)
    column = lax.broadcasted_iota(jnp.int32, (8, 128), 1)

    def solid(row):
        last = pltpu.roll(flags[row : row + 8, 384:512], 64, 1)
        return jnp.where(column < 32, flags[row : row + 8, 0:128], last)

    finish(bank, stress, xface, yface, zface, acc, solid, final)
    for f in range(10):
        for l in range(2):
            for t in range(2):
                rows = slice(8 * t, 8 * t + 8)
                made = final[f, l, 0, rows, :]
                staged[0, f, l, rows, :] = jnp.where(column < 2, made, result[f, l, 0, rows, :])
                made = pltpu.roll(made, 64, 1)
                staged[1, f, l, rows, :] = jnp.where(column >= 126, made, result[f, l, 3, rows, :])
    copies = []
    for side in range(2):
        lanes = slice(384 * side, 384 * side + 128)
        copies.append(pltpu.make_async_copy(staged.at[side], out.at[:, :, :, lanes], sem.at[side]))
        copies[-1].start()
    for copy in copies:
        copy.wait()


def swap(value, axis, offset):
    count = lax.axis_size(axis)
    pairs = []
    for k in range(0, count, 2):
        i, j = (k + offset) % count, (k + offset + 1) % count
        pairs += [(i, j), (j, i)]
    return lax.ppermute(value, axis, pairs)


def local(flow_state, colour_map, cell_flags, probe_weights):
    f32 = jnp.float32
    vmem = pl.BlockSpec(memory_space=pltpu.VMEM)
    hbm = pl.BlockSpec(memory_space=pltpu.HBM)

    def call(kernel, ins, outs, scratch=(), alias={}, cost=0):
        return pl.pallas_call(
            kernel,
            out_shape=[jax.ShapeDtypeStruct(s, d) for s, d, _ in outs],
            in_specs=ins,
            out_specs=[m for _, _, m in outs],
            scratch_shapes=scratch,
            input_output_aliases=alias,
            compiler_params=pltpu.CompilerParams(vmem_limit_bytes=24 * 1024 * 1024),
            cost_estimate=pl.CostEstimate(flops=cost, bytes_accessed=cost, transcendentals=0),
        )

    def banks(n, tiles, rows=ROWS):
        return pltpu.VMEM((n, 2, tiles, rows, 128), f32)

    inputs = [flow_state, colour_map, cell_flags, jnp.transpose(probe_weights, (2, 0, 1))]
    x_near, x_far, flow, colour, flags, weights = call(
        pack_x,
        [hbm] * 4,
        [((24, 512), f32, vmem)] * 2 + [(x.shape, x.dtype, vmem) for x in inputs],
        [pltpu.SemaphoreType.DMA((4,))],
    )(*[pltpu.with_memory_space_constraint(x, pltpu.HBM) for x in inputs])
    x_far = swap(x_far, "gx", 1)
    x_near = swap(x_near, "gx", 0)
    bank, acc, table = call(
        own_cells,
        [vmem] * 3,
        [((FIELDS, 2, 4, ROWS, 128), f32, vmem), ((10, 2, 4, 16, 128), f32, vmem), ((16, 128), f32, vmem)],
        [banks(6, 4), banks(16, 4), banks(10, 4, 16), banks(10, 4, 16)],
        cost=8000000,
    )(flow, colour, weights)
    edge, y_near, y_far = call(
        pack_y,
        [vmem] * 5,
        [((6, 2, 2, ROWS, 128), f32, vmem), ((24, 128), f32, vmem), ((24, 128), f32, vmem)],
    )(flow, colour, x_near, x_far, table)
    y_far = swap(y_far, "gy", 1)
    y_near = swap(y_near, "gy", 0)
    bank, result, out = call(
        whole_rows,
        [vmem] * 6,
        [(bank.shape, f32, vmem), (acc.shape, f32, vmem), ((10, 2, 16, 512), f32, hbm)],
        [banks(24, 4), banks(10, 4), banks(2, 4, 16), pltpu.VMEM((8, 1, 4, 16, 128), f32), pltpu.SemaphoreType.DMA((2,))],
        alias={4: 0, 5: 1},
        cost=8000000,
    )(x_near, x_far, table, flags, bank, acc)
    (out,) = call(
        edge_columns,
        [vmem] * 6 + [hbm],
        [(out.shape, f32, hbm)],
        [
            banks(FIELDS, 1),
            banks(10, 1, 16),
            banks(6, 1),
            banks(16, 1),
            banks(10, 1, 16),
            banks(10, 1, 16),
            banks(24, 1),
            banks(10, 1),
            banks(2, 1, 16),
            pltpu.VMEM((8, 1, 1, 16, 128), f32),
            banks(10, 1, 16),
            pltpu.VMEM((2, 10, 2, 16, 128), f32),
            pltpu.SemaphoreType.DMA((2,)),
        ],
        alias={6: 0},
    )(y_near, y_far, edge, table, flags, result, out)
    return out.reshape(2, 5, 2, 16, 512)


def solution(mesh):
    return jax.shard_map(
        local,
        mesh=mesh,
        in_specs=(P(None, None, "gx", "gy"), P(None, "gx", "gy"), P("gx", "gy"), P()),
        out_specs=P(None, None, None, "gx", "gy"),
        check_vma=False,
    )
```

time: 27.8 us -> 19.8 us (0.71)
  waiting for transfers between devices: 6.96 us -> 2.53 us
  local copies, waits for them, and re-layouts: 1.84 us -> 0 us
  Pallas kernels: 9.24 us -> 7.56 us
    ppermute x4, waiting for transfers between devices: 6.96 us -> 2.53 us  [swap(): return lax.ppermute(value, axis, pairs)]
    unnamed x8 -> x0, local copies, waits for them, and re-layouts: 1.82 us -> none
    pallas_call x3 -> x5, Pallas kernels: 9.24 us -> 7.56 us  [the longest x1 2.86 us: local(): call(whole_rows, [vmem] * 6, [(bank.shape, f32, vmem), (acc.shape, f32, v...]
  transfers between devices with their start and end apart: 4 -> 4, of which waited for: 3 -> 2; matrix products, arithmetic and copies ran while one was open for 0% -> 0% of each run, Pallas kernels for 0% -> 22%
where the time goes in v2:
time: 19.8 us; the launch traced here: 19.7 us
  starting transfers between devices  9.56 us (48%)
  Pallas kernels  7.56 us (38%)
  waiting for transfers between devices  2.53 us (13%)
    ppermute x4, starting transfers between devices, swap(): return lax.ppermute(value, axis, pairs)  9.56 us
    pallas_call x1, Pallas kernels, local(): call(whole_rows, [vmem] * 6, [(bank.shape, f32, vmem), (acc.shape, f32, v...  2.86 us
    ppermute x4, waiting for transfers between devices, swap(): return lax.ppermute(value, axis, pairs)  2.53 us
    pallas_call x1, Pallas kernels, local(): call(edge_columns, [vmem] * 6 + [hbm], [(out.shape, f32, hbm)], [banks(FI...  1.91 us
    pallas_call x1, Pallas kernels, local(): call(own_cells, [vmem] * 3, [((FIELDS, 2, 4, ROWS, 128), f32, vmem), ((10...  1.56 us
    pallas_call x1, Pallas kernels, local(): call(pack_x, [hbm] * 4, [((24, 512), f32, vmem)] * 2 + [(x.shape, x.dtype...  1.05 us
  transfers between devices with their start and end apart: 4, of which 2 were waited for; matrix products, arithmetic and copies ran while one was open for 0% of the time, Pallas kernels for 22%

profile of v2, /device:TPU:56, one launch (start us, length us, event | category | flops | bytes accessed | tf_op | source)
XLA Modules:
  0.0 19.7 jit_solution(6241594963662003674)
XLA Ops:
  0.0 1.1 %shard_map.46 = (f32[24,512]{1,0:T(8,128)S(1)}, f32[24,512]{1,0:T(8,128)S(1)}, f32[5,2,16,512]{3,2,1,0:T(8,128)S(1)}, s32[2,16,512]{2,1,0:T(8,128)S(1)}, s32[16,512]{1,0:T(8,128)S(1)}, /*index=5*/f32[5,2,27]{2,1,0:T(2,128)S(1)}) custom-call(f32[5,2,16,512]{3,2,1,0:T(8,128)} %flow.1, s32[2,16,512]{2,1,0:T(8,128)} %colour.1, s32[16,512]{1,0:T(8,128)} %flags.1, ...), custom_call_target="tpu_custom_call" | custom-call | tf_op jit(solution)/shard_map/pallas_call | solution.py:436
  1.1 0.1 collective-permute-start
  1.2 7.7 %collective-permute-start.1 = (f32[24,512]{1,0:T(8,128)S(1)}, f32[24,512]{1,0:T(8,128)S(1)}, u32[]{:S(2)}, u32[]{:S(2)}) collective-permute-start(f32[24,512]{1,0:T(8,128)S(1)} %get-tuple-element.22), channel_id=1, source_target_pairs={{8,16},{16,8},{24,32},{32,24},{40,48},{48,40},{56,64},{64,56},{72,... | collective-permute-start | bytes 147464 | tf_op jit(solution)/shard_map/ppermute | solution.py:412
  8.9 1.6 %shard_map.47 = (f32[39,2,4,40,128]{4,3,2,1,0:T(8,128)S(1)}, f32[10,2,4,16,128]{4,3,2,1,0:T(8,128)S(1)}, f32[16,128]{1,0:T(8,128)S(1)}) custom-call(f32[5,2,16,512]{3,2,1,0:T(8,128)S(1)} %get-tuple-element.19.flow, s32[2,16,512]{2,1,0:T(8,128)S(1)} %get-tuple-element.20.colour, f32[5,2,27]{2,1,0:T(2,128)S(1)} %get-tuple-element.23.weights), custom_call_target="tpu_custom_call" | custom-call | flops 8000000 | bytes 8000000 | tf_op jit(solution)/shard_map/pallas_call | solution.py:444
  10.4 0.0 collective-permute-done.near
  10.4 0.2 %collective-permute-done.1.far = f32[24,512]{1,0:T(8,128)S(1)} collective-permute-done((f32[24,512]{1,0:T(8,128)S(1)}, f32[24,512]{1,0:T(8,128)S(1)}, u32[]{:S(2)}, u32[]{:S(2)}) %collective-permute-start.1) | collective-permute-done | bytes 49184 | tf_op jit(solution)/shard_map/ppermute | solution.py:412
  10.6 0.2 shard_map.48
  10.8 1.2 %collective-permute-start.2 = (f32[24,128]{1,0:T(8,128)S(1)}, f32[24,128]{1,0:T(8,128)S(1)}, u32[]{:S(2)}, u32[]{:S(2)}) collective-permute-start(f32[24,128]{1,0:T(8,128)S(1)} %get-tuple-element.25), channel_id=1, source_target_pairs={{0,1},{1,0},{2,3},{3,2},{4,5},{5,4},{6,7},{7,6},{8,9},{9,8},{10,11... | collective-permute-start | bytes 36872 | tf_op jit(solution)/shard_map/ppermute | solution.py:412
  12.0 0.6 %collective-permute-start.3 = (f32[24,128]{1,0:T(8,128)S(1)}, f32[24,128]{1,0:T(8,128)S(1)}, u32[]{:S(2)}, u32[]{:S(2)}) collective-permute-start(f32[24,128]{1,0:T(8,128)S(1)} %get-tuple-element.26), channel_id=1, source_target_pairs={{1,2},{2,1},{3,4},{4,3},{5,6},{6,5},{7,0},{0,7},{9,10},{10,9},{11,... | collective-permute-start | bytes 36872 | tf_op jit(solution)/shard_map/ppermute | solution.py:412
  12.6 2.9 %shard_map.49 = (f32[39,2,4,40,128]{4,3,2,1,0:T(8,128)S(1)}, f32[10,2,4,16,128]{4,3,2,1,0:T(8,128)S(1)}, f32[10,2,16,512]{3,2,1,0:T(8,128)}) custom-call(f32[24,512]{1,0:T(8,128)S(1)} %collective-permute-done.near, f32[24,512]{1,0:T(8,128)S(1)} %collective-permute-done.1.far, ...), custom_call_target="tpu_custom_call", output_to_operand_aliasing={{0}: (4, {}), {1}: (5, {})} | custom-call | flops 8000000 | bytes 8000000 | tf_op jit(solution)/shard_map/pallas_call | solution.py:458
  15.5 0.0 collective-permute-done.2.near
  15.5 2.3 %collective-permute-done.3.far = f32[24,128]{1,0:T(8,128)S(1)} collective-permute-done((f32[24,128]{1,0:T(8,128)S(1)}, f32[24,128]{1,0:T(8,128)S(1)}, u32[]{:S(2)}, u32[]{:S(2)}) %collective-permute-start.3) | collective-permute-done | bytes 12320 | tf_op jit(solution)/shard_map/ppermute | solution.py:412
  17.8 1.9 %shard_map.50 = f32[10,2,16,512]{3,2,1,0:T(8,128)} custom-call(f32[24,128]{1,0:T(8,128)S(1)} %collective-permute-done.2.near, f32[24,128]{1,0:T(8,128)S(1)} %collective-permute-done.3.far, f32[6,2,2,40,128]{4,3,2,1,0:T(8,128)S(1)} %get-tuple-element.27.edge, f32[16,128]{1,0:T(8,128)S(1)} %get-tuple-element.24.table, ...), custom_call_target="tpu_custom_call", output_to_operand_aliasing={{}: (6, {})} | custom-call | tf_op jit(solution)/shard_map/pallas_call | solution.py:466
Async XLA Ops:
  1.1 9.4 %collective-permute-start = (f32[24,512]{1,0:T(8,128)S(1)}, f32[24,512]{1,0:T(8,128)S(1)}, u32[]{:S(2)}, u32[]{:S(2)}) collective-permute-start(f32[24,512]{1,0:T(8,128)S(1)} %get-tuple-element.21), channel_id=1, source_target_pairs={{0,8},{8,0},{16,24},{24,16},{32,40},{40,32},{48,56},{56,48},{64,72... | collective-permute-start | bytes 147464 | tf_op jit(solution)/shard_map/ppermute | solution.py:412
  1.2 9.5 %collective-permute-start.1 = (f32[24,512]{1,0:T(8,128)S(1)}, f32[24,512]{1,0:T(8,128)S(1)}, u32[]{:S(2)}, u32[]{:S(2)}) collective-permute-start(f32[24,512]{1,0:T(8,128)S(1)} %get-tuple-element.22), channel_id=1, source_target_pairs={{8,16},{16,8},{24,32},{32,24},{40,48},{48,40},{56,64},{64,56},{72,... | collective-permute-start | bytes 147464 | tf_op jit(solution)/shard_map/ppermute | solution.py:412
  10.8 4.6 %collective-permute-start.2 = (f32[24,128]{1,0:T(8,128)S(1)}, f32[24,128]{1,0:T(8,128)S(1)}, u32[]{:S(2)}, u32[]{:S(2)}) collective-permute-start(f32[24,128]{1,0:T(8,128)S(1)} %get-tuple-element.25), channel_id=1, source_target_pairs={{0,1},{1,0},{2,3},{3,2},{4,5},{5,4},{6,7},{7,6},{8,9},{9,8},{10,11... | collective-permute-start | bytes 36872 | tf_op jit(solution)/shard_map/ppermute | solution.py:412
  12.0 5.8 %collective-permute-start.3 = (f32[24,128]{1,0:T(8,128)S(1)}, f32[24,128]{1,0:T(8,128)S(1)}, u32[]{:S(2)}, u32[]{:S(2)}) collective-permute-start(f32[24,128]{1,0:T(8,128)S(1)} %get-tuple-element.26), channel_id=1, source_target_pairs={{1,2},{2,1},{3,4},{4,3},{5,6},{6,5},{7,0},{0,7},{9,10},{10,9},{11,... | collective-permute-start | bytes 36872 | tf_op jit(solution)/shard_map/ppermute | solution.py:412

commit v3 on v2

--- a/solution.py
+++ b/solution.py
@@ -177,7 +177,7 @@
                     put(xface, 5 * p + v, l, row, made)
 
 
-def finish(bank, stress, xface, yface, zface, acc, flags, out):
+def finish(bank, stress, xface, yface, ypart, zface, acc, flags, emit):
     for t in range(2):
         row = BASE + 8 * t
         for l in range(2):
@@ -190,7 +190,10 @@
             for p in range(2):
                 work = 0.0
                 for e in range(3):
-                    work = work + v_sum[e] * pair(stress, 6 + 9 * p + TENSOR[1][e])
+                    here = get(stress, 6 + 9 * p + TENSOR[1][e], l, row)
+                    after = ahead(here)
+                    put(ypart, 4 * p + e, l, 8 * t, after - ahead(here, -1))
+                    work = work + v_sum[e] * (here + after)
                     work = work + pair(bank, PRIM + 4 + 4 * p + e) * t_sum[e]
                 put(yface, p, l, 8 * t, 0.5 * work)
         both = lambda ref, f: get(ref, f, 0, row) + get(ref, f, 1, row)
@@ -204,31 +207,33 @@
                 work = work + v_sum[e] * dt + both(bank, PRIM + 4 + 4 * p + e) * t_sum[e]
             put(zface, 4 * p + 3, 0, 8 * t, 0.5 * work + both(stress, 6 + 9 * p + 8))
     for t in range(2):
-        row = BASE + 8 * t
-        solid = flags(8 * t) == 1
         for l in range(2):
             for p in range(2):
-                for v in range(5):
+                here = get(stress, 13 + 9 * p, l, BASE + 8 * t)
+                work = get(yface, p, l, 8 * t)
+                put(ypart, 4 * p + 3, l, 8 * t, ahead(here) + work - ahead(here + work, -1))
+    solid = [flags(8 * t) == 1 for t in range(2)]
+    for p in range(2):
+        for v in range(5):
+            for l in range(2):
+                for t in range(2):
+                    row = BASE + 8 * t
                     f = SEED + 5 * p + 1 if v == 0 else FLUX + 4 * p + v - 1
-                    total = get(acc, 5 * p + v, l, 8 * t)
-                    total = total - (8.0 / 12.0) * (get(bank, f, l, row + 1) - get(bank, f, l, row - 1))
-                    total = total + (1.0 / 12.0) * (get(bank, f, l, row + 2) - get(bank, f, l, row - 2))
-                    total = total + get(xface, 5 * p + v, l, row) - get(xface, 5 * p + v, l, row - 1)
+                    near = get(bank, f, l, row + 1) - get(bank, f, l, row - 1)
+                    far = get(bank, f, l, row + 2) - get(bank, f, l, row - 2)
+                    face = get(xface, 5 * p + v, l, row) - get(xface, 5 * p + v, l, row - 1)
+                    total = get(acc, 5 * p + v, l, 8 * t) + face - (8.0 / 12.0) * near + (1.0 / 12.0) * far
                     if v > 0:
                         f = 6 + 9 * p + (6 if v == 4 else TENSOR[0][v - 1])
-                        total = total + get(stress, f, l, row + 1) - get(stress, f, l, row - 1)
-                        here = get(stress, 6 + 9 * p + (7 if v == 4 else TENSOR[1][v - 1]), l, row)
-                        if v == 4:
-                            work = get(yface, p, l, 8 * t)
-                            total = total + ahead(here) + work - ahead(here + work, -1)
-                        else:
-                            total = total + ahead(here) - ahead(here, -1)
+                        viscous = get(stress, f, l, row + 1) - get(stress, f, l, row - 1)
+                        viscous = viscous + get(ypart, 4 * p + v - 1, l, 8 * t)
                         wall = get(zface, 4 * p + v - 1, 0, 8 * t)
-                        total = total + wall if l == 0 else total - wall
-                    put(out, 5 * p + v, l, 8 * t, jnp.where(solid, -get(bank, SEED + 5 * p + v, l, row), total))
-
-
-def pack_x(flow, colour, flags, weights, to_near, to_far, flow_out, colour_out, flags_out, weights_out, sems):
+                        total = total + (viscous + wall if l == 0 else viscous - wall)
+                    value = jnp.where(solid[t], -get(bank, SEED + 5 * p + v, l, row), total)
+                    emit(5 * p + v, l, 8 * t, value)
+
+
+def pack_x(flow, colour, flags, weights, to_far, to_near, flow_out, colour_out, flags_out, weights_out, sems):
     pairs = ((flow, flow_out), (colour, colour_out), (flags, flags_out), (weights, weights_out))
     copies = [pltpu.make_async_copy(src, dst, sems.at[i]) for i, (src, dst) in enumerate(pairs)]
     for copy in copies:
@@ -288,7 +293,7 @@
         fill(far, BASE + 16)
 
 
-def pack_y(flow, colour, near, far, table, edge, to_near, to_far):
+def pack_y(flow, colour, far, near, table, edge, to_far, to_near):
     for l in range(2):
         for side in range(2):
             lanes = slice(384 * side, 384 * side + 128)
@@ -326,7 +331,7 @@
         to_far[...] = right
 
 
-def whole_rows(near, far, table, flags, bank_in, acc, bank, result, out, stress, xface, yface, zface, sem):
+def whole_rows(far, near, table, flags, bank_in, acc, bank, result, stress, xface, yface, ypart, zface):
     def store(v, l, row, src, at):
         for c in range(4):
             bank[STATE + v, l, c, row : row + 2, :] = src[at : at + 2, 128 * c : 128 * c + 128]
@@ -336,21 +341,20 @@
     rows = (BASE - 4, BASE + 4, BASE + 12)
     stresses(bank, stress, rows)
     x_faces(bank, stress, xface, rows)
-    finish(bank, stress, xface, yface, zface, acc, lambda row: flags[row : row + 8, :], result)
-    copies = []
+    solid = lambda row: flags[row : row + 8, :]
+    emit = lambda f, l, row, value: put(result, f, l, row, value)
+    finish(bank, stress, xface, yface, ypart, zface, acc, solid, emit)
+
+
+def edge_columns(
+    far, near, edge, table, flags, result, out, bank, acc, speed_yz, flux_yz, cell, face, stress, xface, yface, ypart,
+    zface, staged, middle_sem, edge_sem,
+):
+    middle = []
     for c in (1, 2):
-        copies.append(
-            pltpu.make_async_copy(result.at[:, :, c], out.at[:, :, :, 128 * c : 128 * c + 128], sem.at[c - 1])
-        )
-        copies[-1].start()
-    for copy in copies:
-        copy.wait()
-
-
-def edge_columns(
-    near, far, edge, table, flags, result, out_in, out, bank, acc, speed_yz, flux_yz, cell, face, stress, xface, yface,
-    zface, final, staged, sem,
-):
+        lanes = slice(128 * c, 128 * c + 128)
+        middle.append(pltpu.make_async_copy(result.at[:, :, c], out.at[:, :, :, lanes], middle_sem.at[c - 1]))
+        middle[-1].start()
     lane = lax.broadcasted_iota(jnp.int32, (24, 128), 1)
     odd = lax.rem(lax.axis_index("gy"), 2)
 
@@ -385,21 +389,20 @@
         last = pltpu.roll(flags[row : row + 8, 384:512], 64, 1)
         return jnp.where(column < 32, flags[row : row + 8, 0:128], last)
 
-    finish(bank, stress, xface, yface, zface, acc, solid, final)
-    for f in range(10):
-        for l in range(2):
-            for t in range(2):
-                rows = slice(8 * t, 8 * t + 8)
-                made = final[f, l, 0, rows, :]
-                staged[0, f, l, rows, :] = jnp.where(column < 2, made, result[f, l, 0, rows, :])
-                made = pltpu.roll(made, 64, 1)
-                staged[1, f, l, rows, :] = jnp.where(column >= 126, made, result[f, l, 3, rows, :])
     copies = []
-    for side in range(2):
-        lanes = slice(384 * side, 384 * side + 128)
-        copies.append(pltpu.make_async_copy(staged.at[side], out.at[:, :, :, lanes], sem.at[side]))
-        copies[-1].start()
-    for copy in copies:
+
+    def emit(f, l, row, made):
+        rows = slice(row, row + 8)
+        staged[0, f, l, rows, :] = jnp.where(column < 2, made, result[f, l, 0, rows, :])
+        staged[1, f, l, rows, :] = jnp.where(column >= 126, pltpu.roll(made, 64, 1), result[f, l, 3, rows, :])
+        if l == 1 and row == 8:
+            for side in range(2):
+                lanes = slice(384 * side, 384 * side + 128)
+                copies.append(pltpu.make_async_copy(staged.at[side, f], out.at[f, :, :, lanes], edge_sem.at[side, f]))
+                copies[-1].start()
+
+    finish(bank, stress, xface, yface, ypart, zface, acc, solid, emit)
+    for copy in middle + copies:
         copy.wait()
 
 
@@ -433,7 +436,7 @@
         return pltpu.VMEM((n, 2, tiles, rows, 128), f32)
 
     inputs = [flow_state, colour_map, cell_flags, jnp.transpose(probe_weights, (2, 0, 1))]
-    x_near, x_far, flow, colour, flags, weights = call(
+    x_far, x_near, flow, colour, flags, weights = call(
         pack_x,
         [hbm] * 4,
         [((24, 512), f32, vmem)] * 2 + [(x.shape, x.dtype, vmem) for x in inputs],
@@ -448,25 +451,25 @@
         [banks(6, 4), banks(16, 4), banks(10, 4, 16), banks(10, 4, 16)],
         cost=8000000,
     )(flow, colour, weights)
-    edge, y_near, y_far = call(
+    edge, y_far, y_near = call(
         pack_y,
         [vmem] * 5,
         [((6, 2, 2, ROWS, 128), f32, vmem), ((24, 128), f32, vmem), ((24, 128), f32, vmem)],
-    )(flow, colour, x_near, x_far, table)
+    )(flow, colour, x_far, x_near, table)
     y_far = swap(y_far, "gy", 1)
     y_near = swap(y_near, "gy", 0)
-    bank, result, out = call(
+    bank, result = call(
         whole_rows,
         [vmem] * 6,
-        [(bank.shape, f32, vmem), (acc.shape, f32, vmem), ((10, 2, 16, 512), f32, hbm)],
-        [banks(24, 4), banks(10, 4), banks(2, 4, 16), pltpu.VMEM((8, 1, 4, 16, 128), f32), pltpu.SemaphoreType.DMA((2,))],
+        [(bank.shape, f32, vmem), (acc.shape, f32, vmem)],
+        [banks(24, 4), banks(10, 4), banks(2, 4, 16), banks(8, 4, 16), pltpu.VMEM((8, 1, 4, 16, 128), f32)],
         alias={4: 0, 5: 1},
         cost=8000000,
-    )(x_near, x_far, table, flags, bank, acc)
+    )(x_far, x_near, table, flags, bank, acc)
     (out,) = call(
         edge_columns,
-        [vmem] * 6 + [hbm],
-        [(out.shape, f32, hbm)],
+        [vmem] * 6,
+        [((10, 2, 16, 512), f32, hbm)],
         [
             banks(FIELDS, 1),
             banks(10, 1, 16),
@@ -477,13 +480,13 @@
             banks(24, 1),
             banks(10, 1),
             banks(2, 1, 16),
+            banks(8, 1, 16),
             pltpu.VMEM((8, 1, 1, 16, 128), f32),
-            banks(10, 1, 16),
             pltpu.VMEM((2, 10, 2, 16, 128), f32),
             pltpu.SemaphoreType.DMA((2,)),
+            pltpu.SemaphoreType.DMA((2, 10)),
         ],
-        alias={6: 0},
-    )(y_near, y_far, edge, table, flags, result, out)
+    )(y_far, y_near, edge, table, flags, result)
     return out.reshape(2, 5, 2, 16, 512)
 
 

time: 19.8 us -> 20.3 us (1.025)
  the two profiles are of different devices: /device:TPU:56 before, /device:TPU:1 now
where the time goes in v3:
time: 20.3 us; the launch traced here: 20.2 us
  starting transfers between devices  12.8 us (63%)
  Pallas kernels  6.95 us (34%)
  waiting for transfers between devices  0.39 us (2%)
    ppermute x4, starting transfers between devices, swap(): return lax.ppermute(value, axis, pairs)  12.8 us
    pallas_call x1, Pallas kernels, local(): call(whole_rows, [vmem] * 6, [(bank.shape, f32, vmem), (acc.shape, f32, v...  2.15 us
    pallas_call x1, Pallas kernels, local(): call(edge_columns, [vmem] * 6, [((10, 2, 16, 512), f32, hbm)], [banks(FIE...  2 us
    pallas_call x1, Pallas kernels, local(): call(own_cells, [vmem] * 3, [((FIELDS, 2, 4, ROWS, 128), f32, vmem), ((10...  1.56 us
    pallas_call x1, Pallas kernels, local(): call(pack_x, [hbm] * 4, [((24, 512), f32, vmem)] * 2 + [(x.shape, x.dtype...  1.05 us
  transfers between devices with their start and end apart: 4, of which 1 were waited for; matrix products, arithmetic and copies ran while one was open for 0% of the time, Pallas kernels for 18%

profile of v3, /device:TPU:1, one launch (start us, length us, event | category | flops | bytes accessed | tf_op | source)
XLA Modules:
  0.0 20.2 jit_solution(13537012520524282194)
XLA Ops:
  0.0 1.1 %shard_map.46 = (f32[24,512]{1,0:T(8,128)S(1)}, f32[24,512]{1,0:T(8,128)S(1)}, f32[5,2,16,512]{3,2,1,0:T(8,128)S(1)}, s32[2,16,512]{2,1,0:T(8,128)S(1)}, s32[16,512]{1,0:T(8,128)S(1)}, /*index=5*/f32[5,2,27]{2,1,0:T(2,128)S(1)}) custom-call(f32[5,2,16,512]{3,2,1,0:T(8,128)} %flow.1, s32[2,16,512]{2,1,0:T(8,128)} %colour.1, s32[16,512]{1,0:T(8,128)} %flags.1, ...), custom_call_target="tpu_custom_call" | custom-call | tf_op jit(solution)/shard_map/pallas_call | solution.py:439
  1.1 4.5 %collective-permute-start = (f32[24,512]{1,0:T(8,128)S(1)}, f32[24,512]{1,0:T(8,128)S(1)}, u32[]{:S(2)}, u32[]{:S(2)}) collective-permute-start(f32[24,512]{1,0:T(8,128)S(1)} %get-tuple-element.20), channel_id=1, source_target_pairs={{8,16},{16,8},{24,32},{32,24},{40,48},{48,40},{56,64},{64,56},{72,... | collective-permute-start | bytes 147464 | tf_op jit(solution)/shard_map/ppermute | solution.py:415
  5.5 5.1 %collective-permute-start.1 = (f32[24,512]{1,0:T(8,128)S(1)}, f32[24,512]{1,0:T(8,128)S(1)}, u32[]{:S(2)}, u32[]{:S(2)}) collective-permute-start(f32[24,512]{1,0:T(8,128)S(1)} %get-tuple-element.21), channel_id=1, source_target_pairs={{0,8},{8,0},{16,24},{24,16},{32,40},{40,32},{48,56},{56,48},{64,72... | collective-permute-start | bytes 147464 | tf_op jit(solution)/shard_map/ppermute | solution.py:415
  10.6 1.6 %shard_map.47 = (f32[39,2,4,40,128]{4,3,2,1,0:T(8,128)S(1)}, f32[10,2,4,16,128]{4,3,2,1,0:T(8,128)S(1)}, f32[16,128]{1,0:T(8,128)S(1)}) custom-call(f32[5,2,16,512]{3,2,1,0:T(8,128)S(1)} %get-tuple-element.18.flow, s32[2,16,512]{2,1,0:T(8,128)S(1)} %get-tuple-element.19.colour, f32[5,2,27]{2,1,0:T(2,128)S(1)} %get-tuple-element.22.weights), custom_call_target="tpu_custom_call" | custom-call | flops 8000000 | bytes 8000000 | tf_op jit(solution)/shard_map/pallas_call | solution.py:447
  12.2 0.0 collective-permute-done.far
  12.2 0.0 collective-permute-done.1.near
  12.2 0.2 shard_map.48
  12.4 3.3 %collective-permute-start.2 = (f32[24,128]{1,0:T(8,128)S(1)}, f32[24,128]{1,0:T(8,128)S(1)}, u32[]{:S(2)}, u32[]{:S(2)}) collective-permute-start(f32[24,128]{1,0:T(8,128)S(1)} %get-tuple-element.24), channel_id=1, source_target_pairs={{1,2},{2,1},{3,4},{4,3},{5,6},{6,5},{7,0},{0,7},{9,10},{10,9},{11,... | collective-permute-start | bytes 36872 | tf_op jit(solution)/shard_map/ppermute | solution.py:415
  15.6 0.0 collective-permute-start.3
  15.6 2.1 %shard_map.49 = (f32[39,2,4,40,128]{4,3,2,1,0:T(8,128)S(1)}, f32[10,2,4,16,128]{4,3,2,1,0:T(8,128)S(1)}) custom-call(f32[24,512]{1,0:T(8,128)S(1)} %collective-permute-done.far, f32[24,512]{1,0:T(8,128)S(1)} %collective-permute-done.1.near, f32[16,128]{1,0:T(8,128)S(1)} %get-tuple-element.23.table, ...), custom_call_target="tpu_custom_call", output_to_operand_aliasing={{0}: (4, {}), {1}: (5, {})} | custom-call | flops 8000000 | bytes 8000000 | tf_op jit(solution)/shard_map/pallas_call | solution.py:461
  17.8 0.0 collective-permute-done.2.far
  17.8 0.4 %collective-permute-done.3.near = f32[24,128]{1,0:T(8,128)S(1)} collective-permute-done((f32[24,128]{1,0:T(8,128)S(1)}, f32[24,128]{1,0:T(8,128)S(1)}, u32[]{:S(2)}, u32[]{:S(2)}) %collective-permute-start.3) | collective-permute-done | bytes 12320 | tf_op jit(solution)/shard_map/ppermute | solution.py:415
  18.2 2.0 %shard_map.50 = f32[10,2,16,512]{3,2,1,0:T(8,128)} custom-call(f32[24,128]{1,0:T(8,128)S(1)} %collective-permute-done.2.far, f32[24,128]{1,0:T(8,128)S(1)} %collective-permute-done.3.near, f32[6,2,2,40,128]{4,3,2,1,0:T(8,128)S(1)} %get-tuple-element.26.edge, f32[16,128]{1,0:T(8,128)S(1)} %get-tuple-element.23.table, s32[16,512]{1,0:T(8,128)S(1)} %get-tuple-element.27.flags, ...), custom_call_target="tpu_custom_call" | custom-call | tf_op jit(solution)/shard_map/pallas_call | solution.py:469
Async XLA Ops:
  1.1 11.1 %collective-permute-start = (f32[24,512]{1,0:T(8,128)S(1)}, f32[24,512]{1,0:T(8,128)S(1)}, u32[]{:S(2)}, u32[]{:S(2)}) collective-permute-start(f32[24,512]{1,0:T(8,128)S(1)} %get-tuple-element.20), channel_id=1, source_target_pairs={{8,16},{16,8},{24,32},{32,24},{40,48},{48,40},{56,64},{64,56},{72,... | collective-permute-start | bytes 147464 | tf_op jit(solution)/shard_map/ppermute | solution.py:415
  5.5 6.6 %collective-permute-start.1 = (f32[24,512]{1,0:T(8,128)S(1)}, f32[24,512]{1,0:T(8,128)S(1)}, u32[]{:S(2)}, u32[]{:S(2)}) collective-permute-start(f32[24,512]{1,0:T(8,128)S(1)} %get-tuple-element.21), channel_id=1, source_target_pairs={{0,8},{8,0},{16,24},{24,16},{32,40},{40,32},{48,56},{56,48},{64,72... | collective-permute-start | bytes 147464 | tf_op jit(solution)/shard_map/ppermute | solution.py:415
  12.4 5.4 %collective-permute-start.2 = (f32[24,128]{1,0:T(8,128)S(1)}, f32[24,128]{1,0:T(8,128)S(1)}, u32[]{:S(2)}, u32[]{:S(2)}) collective-permute-start(f32[24,128]{1,0:T(8,128)S(1)} %get-tuple-element.24), channel_id=1, source_target_pairs={{1,2},{2,1},{3,4},{4,3},{5,6},{6,5},{7,0},{0,7},{9,10},{10,9},{11,... | collective-permute-start | bytes 36872 | tf_op jit(solution)/shard_map/ppermute | solution.py:415
  15.6 2.5 %collective-permute-start.3 = (f32[24,128]{1,0:T(8,128)S(1)}, f32[24,128]{1,0:T(8,128)S(1)}, u32[]{:S(2)}, u32[]{:S(2)}) collective-permute-start(f32[24,128]{1,0:T(8,128)S(1)} %get-tuple-element.25), channel_id=1, source_target_pairs={{0,1},{1,0},{2,3},{3,2},{4,5},{5,4},{6,7},{7,6},{8,9},{9,8},{10,11... | collective-permute-start | bytes 36872 | tf_op jit(solution)/shard_map/ppermute | solution.py:415

commit v4 on v3

--- a/solution.py
+++ b/solution.py
@@ -86,7 +86,8 @@
 
 
 def inviscid_yz(bank, speed_yz, flux_yz, cell, face, acc):
-    places = [(l, t) for l in range(2) for t in range(2)]
+    count = acc.shape[3] // 8
+    places = [(l, t) for l in range(2) for t in range(count)]
     for l, t in places:
         row = BASE + 8 * t
         for p in range(2):
@@ -112,7 +113,7 @@
                 central = get(cell, 5 * p + v, l, 8 * t)
                 made = ds[p] * jump + s_sum * (ahead(here) - here) - (central + ahead(central))
                 put(face, 5 * p + v, l, 8 * t, made)
-    for t in range(2):
+    for t in range(count):
         row = BASE + 8 * t
         s_sum = get(speed_yz, 3, 0, row) + get(speed_yz, 3, 1, row)
         ds = [get(speed_yz, 4 + p, 0, row) + get(speed_yz, 4 + p, 1, row) for p in range(2)]
@@ -178,7 +179,8 @@
 
 
 def finish(bank, stress, xface, yface, ypart, zface, acc, flags, emit):
-    for t in range(2):
+    count = acc.shape[3] // 8
+    for t in range(count):
         row = BASE + 8 * t
         for l in range(2):
             def pair(ref, f):
@@ -206,17 +208,17 @@
                 put(zface, 4 * p + e, 0, 8 * t, dt)
                 work = work + v_sum[e] * dt + both(bank, PRIM + 4 + 4 * p + e) * t_sum[e]
             put(zface, 4 * p + 3, 0, 8 * t, 0.5 * work + both(stress, 6 + 9 * p + 8))
-    for t in range(2):
+    for t in range(count):
         for l in range(2):
             for p in range(2):
                 here = get(stress, 13 + 9 * p, l, BASE + 8 * t)
                 work = get(yface, p, l, 8 * t)
                 put(ypart, 4 * p + 3, l, 8 * t, ahead(here) + work - ahead(here + work, -1))
-    solid = [flags(8 * t) == 1 for t in range(2)]
+    solid = [flags(8 * t) == 1 for t in range(count)]
     for p in range(2):
         for v in range(5):
             for l in range(2):
-                for t in range(2):
+                for t in range(count):
                     row = BASE + 8 * t
                     f = SEED + 5 * p + 1 if v == 0 else FLUX + 4 * p + v - 1
                     near = get(bank, f, l, row + 1) - get(bank, f, l, row - 1)
@@ -233,7 +235,7 @@
                     emit(5 * p + v, l, 8 * t, value)
 
 
-def pack_x(flow, colour, flags, weights, to_far, to_near, flow_out, colour_out, flags_out, weights_out, sems):
+def pack_x(flow, colour, flags, weights, to_near, to_far, flow_out, colour_out, flags_out, weights_out, sems):
     pairs = ((flow, flow_out), (colour, colour_out), (flags, flags_out), (weights, weights_out))
     copies = [pltpu.make_async_copy(src, dst, sems.at[i]) for i, (src, dst) in enumerate(pairs)]
     for copy in copies:
@@ -259,7 +261,10 @@
         fill(to_far, 14)
 
 
-def own_cells(flow, colour, weights, bank, acc, table, speed_yz, flux_yz, cell, face):
+def own_cells(
+    flow, colour, weights, flags, acc, table, result, bank, speed_yz, flux_yz, cell, face, stress, xface, yface, ypart,
+    zface,
+):
     for p in range(2):
         for v in range(5):
             line = weights[v, p : p + 1, :]
@@ -272,9 +277,14 @@
             bank[STATE + 5, l, c, BASE : BASE + 16, :] = colour[l, :, lanes].astype(jnp.float32)
     pointwise(bank, table, (BASE, BASE + 8), speed_yz, flux_yz)
     inviscid_yz(bank, speed_yz, flux_yz, cell, face, acc)
-
-
-def x_halo(near, far, store):
+    stresses(bank, stress, (BASE, BASE + 8))
+    x_faces(bank, stress, xface, (BASE, BASE + 8))
+    solid = lambda row: flags[row : row + 8, :]
+    emit = lambda f, l, row, value: put(result, f, l, row, value)
+    finish(bank, stress, xface, yface, ypart, zface, acc, solid, emit)
+
+
+def x_halo(near, far, store, above=BASE + 16):
     odd = lax.rem(lax.axis_index("gx"), 2)
 
     def fill(src, row):
@@ -285,15 +295,15 @@
     @pl.when(odd == 0)
     def _():
         fill(far, BASE - 2)
-        fill(near, BASE + 16)
+        fill(near, above)
 
     @pl.when(odd == 1)
     def _():
         fill(near, BASE - 2)
-        fill(far, BASE + 16)
-
-
-def pack_y(flow, colour, far, near, table, edge, to_far, to_near):
+        fill(far, above)
+
+
+def pack_y(flow, colour, near, far, table, edge, to_far, to_near):
     for l in range(2):
         for side in range(2):
             lanes = slice(384 * side, 384 * side + 128)
@@ -331,18 +341,38 @@
         to_far[...] = right
 
 
-def whole_rows(far, near, table, flags, bank_in, acc, bank, result, stress, xface, yface, ypart, zface):
+def edge_rows(
+    near, far, flow, colour, table, flags, whole, result_in, result, bank, acc, stress, xface, yface, ypart, zface
+):
+    for l in range(2):
+        for c in range(4):
+            lanes = slice(128 * c, 128 * c + 128)
+            for first, row in ((0, BASE), (12, BASE + 4)):
+                for v in range(5):
+                    bank[STATE + v, l, c, row : row + 4, :] = flow[v, l, first : first + 4, lanes]
+                bank[STATE + 5, l, c, row : row + 4, :] = colour[l, first : first + 4, lanes].astype(jnp.float32)
+
     def store(v, l, row, src, at):
         for c in range(4):
             bank[STATE + v, l, c, row : row + 2, :] = src[at : at + 2, 128 * c : 128 * c + 128]
 
-    x_halo(near, far, store)
-    pointwise(bank, table, (BASE - 4, BASE + 12))
-    rows = (BASE - 4, BASE + 4, BASE + 12)
+    x_halo(near, far, store, BASE + 8)
+    rows = (BASE - 4, BASE + 4)
+    pointwise(bank, table, rows)
     stresses(bank, stress, rows)
     x_faces(bank, stress, xface, rows)
-    solid = lambda row: flags[row : row + 8, :]
-    emit = lambda f, l, row, value: put(result, f, l, row, value)
+    upper = lax.broadcasted_iota(jnp.int32, (8, 512), 0) < 4
+    for f in range(10):
+        for l in range(2):
+            put(acc, f, l, 0, jnp.where(upper, get(whole, f, l, 0), get(whole, f, l, 8)))
+
+    def emit(f, l, row, made):
+        for c in range(4):
+            lanes = slice(128 * c, 128 * c + 128)
+            result[f, l, c, 0:2, :] = made[0:2, lanes]
+            result[f, l, c, 14:16, :] = made[6:8, lanes]
+
+    solid = lambda row: jnp.where(upper, flags[0:8, :], flags[8:16, :])
     finish(bank, stress, xface, yface, ypart, zface, acc, solid, emit)
 
 
@@ -436,7 +466,7 @@
         return pltpu.VMEM((n, 2, tiles, rows, 128), f32)
 
     inputs = [flow_state, colour_map, cell_flags, jnp.transpose(probe_weights, (2, 0, 1))]
-    x_far, x_near, flow, colour, flags, weights = call(
+    x_near, x_far, flow, colour, flags, weights = call(
         pack_x,
         [hbm] * 4,
         [((24, 512), f32, vmem)] * 2 + [(x.shape, x.dtype, vmem) for x in inputs],
@@ -444,28 +474,48 @@
     )(*[pltpu.with_memory_space_constraint(x, pltpu.HBM) for x in inputs])
     x_far = swap(x_far, "gx", 1)
     x_near = swap(x_near, "gx", 0)
-    bank, acc, table = call(
+    plane = (10, 2, 4, 16, 128)
+    acc, table, result = call(
         own_cells,
-        [vmem] * 3,
-        [((FIELDS, 2, 4, ROWS, 128), f32, vmem), ((10, 2, 4, 16, 128), f32, vmem), ((16, 128), f32, vmem)],
-        [banks(6, 4), banks(16, 4), banks(10, 4, 16), banks(10, 4, 16)],
+        [vmem] * 4,
+        [(plane, f32, vmem), ((16, 128), f32, vmem), (plane, f32, vmem)],
+        [
+            banks(FIELDS, 4),
+            banks(6, 4),
+            banks(16, 4),
+            banks(10, 4, 16),
+            banks(10, 4, 16),
+            banks(24, 4),
+            banks(10, 4),
+            banks(2, 4, 16),
+            banks(8, 4, 16),
+            pltpu.VMEM((8, 1, 4, 16, 128), f32),
+        ],
         cost=8000000,
-    )(flow, colour, weights)
+    )(flow, colour, weights, flags)
     edge, y_far, y_near = call(
         pack_y,
         [vmem] * 5,
         [((6, 2, 2, ROWS, 128), f32, vmem), ((24, 128), f32, vmem), ((24, 128), f32, vmem)],
-    )(flow, colour, x_far, x_near, table)
+    )(flow, colour, x_near, x_far, table)
     y_far = swap(y_far, "gy", 1)
     y_near = swap(y_near, "gy", 0)
-    bank, result = call(
-        whole_rows,
-        [vmem] * 6,
-        [(bank.shape, f32, vmem), (acc.shape, f32, vmem)],
-        [banks(24, 4), banks(10, 4), banks(2, 4, 16), banks(8, 4, 16), pltpu.VMEM((8, 1, 4, 16, 128), f32)],
-        alias={4: 0, 5: 1},
+    (result,) = call(
+        edge_rows,
+        [vmem] * 8,
+        [(plane, f32, vmem)],
+        [
+            banks(FIELDS, 4),
+            banks(10, 4, 8),
+            banks(24, 4),
+            banks(10, 4),
+            banks(2, 4, 8),
+            banks(8, 4, 8),
+            pltpu.VMEM((8, 1, 4, 8, 128), f32),
+        ],
+        alias={7: 0},
         cost=8000000,
-    )(x_far, x_near, table, flags, bank, acc)
+    )(x_near, x_far, flow, colour, table, flags, acc, result)
     (out,) = call(
         edge_columns,
         [vmem] * 6,

time: 20.3 us -> 20.5 us (level)
  the two profiles are of different devices: /device:TPU:1 before, /device:TPU:32 now
where the time goes in v4:
time: 20.5 us; the launch traced here: 20.4 us
  starting transfers between devices  12.4 us (60%)
  Pallas kernels  7.71 us (38%)
  waiting for transfers between devices  0.27 us (1%)
    ppermute x4, starting transfers between devices, swap(): return lax.ppermute(value, axis, pairs)  12.4 us
    pallas_call x1, Pallas kernels, local(): call(own_cells, [vmem] * 4, [(plane, f32, vmem), ((16, 128), f32, vmem),...  2.95 us
    pallas_call x1, Pallas kernels, local(): call(edge_columns, [vmem] * 6, [((10, 2, 16, 512), f32, hbm)], [banks(FIE...  2.01 us
    pallas_call x1, Pallas kernels, local(): call(edge_rows, [vmem] * 8, [(plane, f32, vmem)], [banks(FIELDS, 4), bank...  1.52 us
    pallas_call x1, Pallas kernels, local(): call(pack_x, [hbm] * 4, [((24, 512), f32, vmem)] * 2 + [(x.shape, x.dtype...  1.06 us
  transfers between devices with their start and end apart: 4, of which 1 were waited for; matrix products, arithmetic and copies ran while one was open for 0% of the time, Pallas kernels for 22%

profile of v4, /device:TPU:32, one launch (start us, length us, event | category | flops | bytes accessed | tf_op | source)
XLA Modules:
  0.0 20.4 jit_solution(15124005817905062441)
XLA Ops:
  0.0 1.1 %shard_map.46 = (f32[24,512]{1,0:T(8,128)S(1)}, f32[24,512]{1,0:T(8,128)S(1)}, f32[5,2,16,512]{3,2,1,0:T(8,128)S(1)}, s32[2,16,512]{2,1,0:T(8,128)S(1)}, s32[16,512]{1,0:T(8,128)S(1)}, /*index=5*/f32[5,2,27]{2,1,0:T(2,128)S(1)}) custom-call(f32[5,2,16,512]{3,2,1,0:T(8,128)} %flow.1, s32[2,16,512]{2,1,0:T(8,128)} %colour.1, s32[16,512]{1,0:T(8,128)} %flags.1, ...), custom_call_target="tpu_custom_call" | custom-call | tf_op jit(solution)/shard_map/pallas_call | solution.py:469
  1.1 0.1 collective-permute-start
  1.2 7.7 %collective-permute-start.1 = (f32[24,512]{1,0:T(8,128)S(1)}, f32[24,512]{1,0:T(8,128)S(1)}, u32[]{:S(2)}, u32[]{:S(2)}) collective-permute-start(f32[24,512]{1,0:T(8,128)S(1)} %get-tuple-element.20), channel_id=1, source_target_pairs={{8,16},{16,8},{24,32},{32,24},{40,48},{48,40},{56,64},{64,56},{72,... | collective-permute-start | bytes 147464 | tf_op jit(solution)/shard_map/ppermute | solution.py:445
  8.9 3.0 %shard_map.47 = (f32[10,2,4,16,128]{4,3,2,1,0:T(8,128)S(1)}, f32[16,128]{1,0:T(8,128)S(1)}, f32[10,2,4,16,128]{4,3,2,1,0:T(8,128)S(1)}) custom-call(f32[5,2,16,512]{3,2,1,0:T(8,128)S(1)} %get-tuple-element.17.flow, s32[2,16,512]{2,1,0:T(8,128)S(1)} %get-tuple-element.18.colour, f32[5,2,27]{2,1,0:T(2,128)S(1)} %get-tuple-element.21.weights, ...), custom_call_target="tpu_custom_call" | custom-call | flops 8000000 | bytes 8000000 | tf_op jit(solution)/shard_map/pallas_call | solution.py:478
  11.8 0.0 collective-permute-done.near
  11.8 0.0 collective-permute-done.1.far
  11.8 0.2 shard_map.48
  12.0 2.1 %collective-permute-start.2 = (f32[24,128]{1,0:T(8,128)S(1)}, f32[24,128]{1,0:T(8,128)S(1)}, u32[]{:S(2)}, u32[]{:S(2)}) collective-permute-start(f32[24,128]{1,0:T(8,128)S(1)} %get-tuple-element.24), channel_id=1, source_target_pairs={{1,2},{2,1},{3,4},{4,3},{5,6},{6,5},{7,0},{0,7},{9,10},{10,9},{11,... | collective-permute-start | bytes 36872 | tf_op jit(solution)/shard_map/ppermute | solution.py:445
  14.1 2.5 %collective-permute-start.3 = (f32[24,128]{1,0:T(8,128)S(1)}, f32[24,128]{1,0:T(8,128)S(1)}, u32[]{:S(2)}, u32[]{:S(2)}) collective-permute-start(f32[24,128]{1,0:T(8,128)S(1)} %get-tuple-element.25), channel_id=1, source_target_pairs={{0,1},{1,0},{2,3},{3,2},{4,5},{5,4},{6,7},{7,6},{8,9},{9,8},{10,11... | collective-permute-start | bytes 36872 | tf_op jit(solution)/shard_map/ppermute | solution.py:445
  16.6 1.5 %shard_map.49.result = f32[10,2,4,16,128]{4,3,2,1,0:T(8,128)S(1)} custom-call(f32[24,512]{1,0:T(8,128)S(1)} %collective-permute-done.near, f32[24,512]{1,0:T(8,128)S(1)} %collective-permute-done.1.far, f32[5,2,16,512]{3,2,1,0:T(8,128)S(1)} %get-tuple-element.17.flow, s32[2,16,512]{2,1,0:T(8,128)S(1)} %get-tuple-element.18.colour, ...), custom_call_target="tpu_custom_call", output_to_operand_aliasing={{}: (7, {})} | custom-call | flops 8000000 | bytes 8000000 | tf_op jit(solution)/shard_map/pallas_call | solution.py:503
  18.1 0.0 collective-permute-done.2.far
  18.1 0.3 %collective-permute-done.3.near = f32[24,128]{1,0:T(8,128)S(1)} collective-permute-done((f32[24,128]{1,0:T(8,128)S(1)}, f32[24,128]{1,0:T(8,128)S(1)}, u32[]{:S(2)}, u32[]{:S(2)}) %collective-permute-start.3) | collective-permute-done | bytes 12320 | tf_op jit(solution)/shard_map/ppermute | solution.py:445
  18.4 2.0 %shard_map.50 = f32[10,2,16,512]{3,2,1,0:T(8,128)} custom-call(f32[24,128]{1,0:T(8,128)S(1)} %collective-permute-done.2.far, f32[24,128]{1,0:T(8,128)S(1)} %collective-permute-done.3.near, f32[6,2,2,40,128]{4,3,2,1,0:T(8,128)S(1)} %get-tuple-element.26.edge, f32[16,128]{1,0:T(8,128)S(1)} %get-tuple-element.23.table, s32[16,512]{1,0:T(8,128)S(1)} %get-tuple-element.22.flags, ...), custom_call_target="tpu_custom_call" | custom-call | tf_op jit(solution)/shard_map/pallas_call | solution.py:519
Async XLA Ops:
  1.1 10.8 %collective-permute-start = (f32[24,512]{1,0:T(8,128)S(1)}, f32[24,512]{1,0:T(8,128)S(1)}, u32[]{:S(2)}, u32[]{:S(2)}) collective-permute-start(f32[24,512]{1,0:T(8,128)S(1)} %get-tuple-element.19), channel_id=1, source_target_pairs={{0,8},{8,0},{16,24},{24,16},{32,40},{40,32},{48,56},{56,48},{64,72... | collective-permute-start | bytes 147464 | tf_op jit(solution)/shard_map/ppermute | solution.py:445
  1.2 10.7 %collective-permute-start.1 = (f32[24,512]{1,0:T(8,128)S(1)}, f32[24,512]{1,0:T(8,128)S(1)}, u32[]{:S(2)}, u32[]{:S(2)}) collective-permute-start(f32[24,512]{1,0:T(8,128)S(1)} %get-tuple-element.20), channel_id=1, source_target_pairs={{8,16},{16,8},{24,32},{32,24},{40,48},{48,40},{56,64},{64,56},{72,... | collective-permute-start | bytes 147464 | tf_op jit(solution)/shard_map/ppermute | solution.py:445
  12.0 6.1 %collective-permute-start.2 = (f32[24,128]{1,0:T(8,128)S(1)}, f32[24,128]{1,0:T(8,128)S(1)}, u32[]{:S(2)}, u32[]{:S(2)}) collective-permute-start(f32[24,128]{1,0:T(8,128)S(1)} %get-tuple-element.24), channel_id=1, source_target_pairs={{1,2},{2,1},{3,4},{4,3},{5,6},{6,5},{7,0},{0,7},{9,10},{10,9},{11,... | collective-permute-start | bytes 36872 | tf_op jit(solution)/shard_map/ppermute | solution.py:445
  14.1 4.3 %collective-permute-start.3 = (f32[24,128]{1,0:T(8,128)S(1)}, f32[24,128]{1,0:T(8,128)S(1)}, u32[]{:S(2)}, u32[]{:S(2)}) collective-permute-start(f32[24,128]{1,0:T(8,128)S(1)} %get-tuple-element.25), channel_id=1, source_target_pairs={{0,1},{1,0},{2,3},{3,2},{4,5},{5,4},{6,7},{7,6},{8,9},{9,8},{10,11... | collective-permute-start | bytes 36872 | tf_op jit(solution)/shard_map/ppermute | solution.py:445

commit v5 on v3

--- a/solution.py
+++ b/solution.py
@@ -27,11 +27,11 @@
     return pltpu.roll(value, (-step) % value.shape[1], 1)
 
 
-def pointwise(bank, table, rows, speed_yz=None, flux_yz=None):
+def pointwise(bank, table, rows, height, speed_yz=None, flux_yz=None):
     for l in range(2):
         for row in rows:
             for c in range(bank.shape[2]):
-                at = (l, c, slice(row, row + 8), slice(None))
+                at = (l, c, slice(row, row + height), slice(None))
                 u = [bank[(STATE + v,) + at] for v in range(5)]
                 shade = bank[(STATE + 5,) + at].astype(jnp.int32) & 127
                 r = 1.0 / u[0]
@@ -56,7 +56,7 @@
                 for p in range(2):
                     d = []
                     for v in range(5):
-                        line = jnp.broadcast_to(table[5 * p + v : 5 * p + v + 1, :], (8, 128))
+                        line = jnp.broadcast_to(table[5 * p + v : 5 * p + v + 1, :], (height, 128))
                         d.append(jnp.take_along_axis(line, shade, axis=1, mode="promise_in_bounds"))
                         bank[(SEED + 5 * p + v,) + at] = d[v]
                     dvel = [(d[1 + e] - vel[e] * d[0]) * r for e in range(3)]
@@ -86,7 +86,8 @@
 
 
 def inviscid_yz(bank, speed_yz, flux_yz, cell, face, acc):
-    places = [(l, t) for l in range(2) for t in range(2)]
+    count = acc.shape[3] // 8
+    places = [(l, t) for l in range(2) for t in range(count)]
     for l, t in places:
         row = BASE + 8 * t
         for p in range(2):
@@ -112,7 +113,7 @@
                 central = get(cell, 5 * p + v, l, 8 * t)
                 made = ds[p] * jump + s_sum * (ahead(here) - here) - (central + ahead(central))
                 put(face, 5 * p + v, l, 8 * t, made)
-    for t in range(2):
+    for t in range(count):
         row = BASE + 8 * t
         s_sum = get(speed_yz, 3, 0, row) + get(speed_yz, 3, 1, row)
         ds = [get(speed_yz, 4 + p, 0, row) + get(speed_yz, 4 + p, 1, row) for p in range(2)]
@@ -178,7 +179,8 @@
 
 
 def finish(bank, stress, xface, yface, ypart, zface, acc, flags, emit):
-    for t in range(2):
+    count = acc.shape[3] // 8
+    for t in range(count):
         row = BASE + 8 * t
         for l in range(2):
             def pair(ref, f):
@@ -206,17 +208,17 @@
                 put(zface, 4 * p + e, 0, 8 * t, dt)
                 work = work + v_sum[e] * dt + both(bank, PRIM + 4 + 4 * p + e) * t_sum[e]
             put(zface, 4 * p + 3, 0, 8 * t, 0.5 * work + both(stress, 6 + 9 * p + 8))
-    for t in range(2):
+    for t in range(count):
         for l in range(2):
             for p in range(2):
                 here = get(stress, 13 + 9 * p, l, BASE + 8 * t)
                 work = get(yface, p, l, 8 * t)
                 put(ypart, 4 * p + 3, l, 8 * t, ahead(here) + work - ahead(here + work, -1))
-    solid = [flags(8 * t) == 1 for t in range(2)]
+    solid = [flags(8 * t) == 1 for t in range(count)]
     for p in range(2):
         for v in range(5):
             for l in range(2):
-                for t in range(2):
+                for t in range(count):
                     row = BASE + 8 * t
                     f = SEED + 5 * p + 1 if v == 0 else FLUX + 4 * p + v - 1
                     near = get(bank, f, l, row + 1) - get(bank, f, l, row - 1)
@@ -233,7 +235,7 @@
                     emit(5 * p + v, l, 8 * t, value)
 
 
-def pack_x(flow, colour, flags, weights, to_far, to_near, flow_out, colour_out, flags_out, weights_out, sems):
+def pack_x(flow, colour, flags, weights, to_near, to_far, flow_out, colour_out, flags_out, weights_out, sems):
     pairs = ((flow, flow_out), (colour, colour_out), (flags, flags_out), (weights, weights_out))
     copies = [pltpu.make_async_copy(src, dst, sems.at[i]) for i, (src, dst) in enumerate(pairs)]
     for copy in copies:
@@ -270,7 +272,7 @@
             for v in range(5):
                 bank[STATE + v, l, c, BASE : BASE + 16, :] = flow[v, l, :, lanes]
             bank[STATE + 5, l, c, BASE : BASE + 16, :] = colour[l, :, lanes].astype(jnp.float32)
-    pointwise(bank, table, (BASE, BASE + 8), speed_yz, flux_yz)
+    pointwise(bank, table, (BASE, BASE + 8), 8, speed_yz, flux_yz)
     inviscid_yz(bank, speed_yz, flux_yz, cell, face, acc)
 
 
@@ -293,7 +295,14 @@
         fill(far, BASE + 16)
 
 
-def pack_y(flow, colour, far, near, table, edge, to_far, to_near):
+def fold(first, last):
+    rows = first.shape[0] - 8
+    lane = lax.broadcasted_iota(jnp.int32, first.shape, 1)
+    made = jnp.where(lane < 64, pltpu.roll(first, 32, 1), last)
+    return jnp.where((lane[:rows] >= 48) & (lane[:rows] < 112), pltpu.roll(made[8:], 64, 1), made[:rows])
+
+
+def pack_y(flow, colour, near, far, table, strip, to_far, to_near, edge):
     for l in range(2):
         for side in range(2):
             lanes = slice(384 * side, 384 * side + 128)
@@ -315,8 +324,12 @@
                 at = 2 * (6 * l + v)
                 moved = pltpu.roll(edge[v, l, side, BASE - 4 : BASE + 20, :], (at - first) % 128, 1)
                 made = jnp.where((lane >= at) & (lane < at + 2), moved, made)
-        return made
-
+        return jnp.where(lane[:16] < 64, made[:16], pltpu.roll(made[8:], 64, 1))
+
+    for v in range(6):
+        for l in range(2):
+            span = slice(BASE - 4, BASE + 20)
+            strip[v, l] = fold(edge[v, l, 0, span, :], edge[v, l, 1, span, :])
     left, right = columns(0, 0), columns(1, 126)
     odd = lax.rem(lax.axis_index("gy"), 2)
 
@@ -331,13 +344,13 @@
         to_far[...] = right
 
 
-def whole_rows(far, near, table, flags, bank_in, acc, bank, result, stress, xface, yface, ypart, zface):
+def whole_rows(near, far, table, flags, bank_in, acc, bank, result, stress, xface, yface, ypart, zface):
     def store(v, l, row, src, at):
         for c in range(4):
             bank[STATE + v, l, c, row : row + 2, :] = src[at : at + 2, 128 * c : 128 * c + 128]
 
     x_halo(near, far, store)
-    pointwise(bank, table, (BASE - 4, BASE + 12))
+    pointwise(bank, table, (BASE - 4, BASE + 12), 8)
     rows = (BASE - 4, BASE + 4, BASE + 12)
     stresses(bank, stress, rows)
     x_faces(bank, stress, xface, rows)
@@ -347,7 +360,7 @@
 
 
 def edge_columns(
-    far, near, edge, table, flags, result, out, bank, acc, speed_yz, flux_yz, cell, face, stress, xface, yface, ypart,
+    far, near, strip, table, flags, result, out, bank, acc, speed_yz, flux_yz, cell, face, stress, xface, yface, ypart,
     zface, staged, middle_sem, edge_sem,
 ):
     middle = []
@@ -355,20 +368,17 @@
         lanes = slice(128 * c, 128 * c + 128)
         middle.append(pltpu.make_async_copy(result.at[:, :, c], out.at[:, :, :, lanes], middle_sem.at[c - 1]))
         middle[-1].start()
-    lane = lax.broadcasted_iota(jnp.int32, (24, 128), 1)
+    lane = lax.broadcasted_iota(jnp.int32, (16, 128), 1)
+    place = lane & 63
     odd = lax.rem(lax.axis_index("gy"), 2)
 
     def unpack(low, high):
         for l in range(2):
             for v in range(6):
                 at = 2 * (6 * l + v)
-                first = edge[v, l, 0, BASE - 4 : BASE + 20, :]
-                last = pltpu.roll(edge[v, l, 1, BASE - 4 : BASE + 20, :], 64, 1)
-                below = pltpu.roll(low[...], (126 - at) % 128, 1)
-                above = pltpu.roll(high[...], 64 - at, 1)
-                made = jnp.where(lane < 32, first, last)
-                made = jnp.where(lane >= 64, above, made)
-                bank[STATE + v, l, 0, BASE - 4 : BASE + 20, :] = jnp.where(lane >= 96, below, made)
+                made = jnp.where(place < 2, pltpu.roll(high[...], (-at) % 128, 1), strip[v, l])
+                made = jnp.where((place == 30) | (place == 31), pltpu.roll(low[...], 30 - at, 1), made)
+                bank[STATE + v, l, 0, BASE - 4 : BASE + 12, :] = made
 
     @pl.when(odd == 0)
     def _():
@@ -378,24 +388,23 @@
     def _():
         unpack(near, far)
 
-    rows = (BASE - 4, BASE + 4, BASE + 12)
-    pointwise(bank, table, rows, speed_yz, flux_yz)
+    rows = (BASE - 4, BASE + 4)
+    pointwise(bank, table, (BASE - 4,), 16, speed_yz, flux_yz)
     inviscid_yz(bank, speed_yz, flux_yz, cell, face, acc)
     stresses(bank, stress, rows)
     x_faces(bank, stress, xface, rows)
-    column = lax.broadcasted_iota(jnp.int32, (8, 128), 1)
-
-    def solid(row):
-        last = pltpu.roll(flags[row : row + 8, 384:512], 64, 1)
-        return jnp.where(column < 32, flags[row : row + 8, 0:128], last)
-
+    column = lane[:8]
+    solid = lambda row: fold(flags[:, 0:128], flags[:, 384:512])
     copies = []
 
     def emit(f, l, row, made):
-        rows = slice(row, row + 8)
-        staged[0, f, l, rows, :] = jnp.where(column < 2, made, result[f, l, 0, rows, :])
-        staged[1, f, l, rows, :] = jnp.where(column >= 126, pltpu.roll(made, 64, 1), result[f, l, 3, rows, :])
-        if l == 1 and row == 8:
+        top, low = slice(0, 8), slice(8, 16)
+        half, rest = pltpu.roll(made, 64, 1), pltpu.roll(made, 32, 1)
+        staged[0, f, l, top, :] = jnp.where(column < 2, pltpu.roll(made, 96, 1), result[f, l, 0, top, :])
+        staged[0, f, l, low, :] = jnp.where(column < 2, rest, result[f, l, 0, low, :])
+        staged[1, f, l, top, :] = jnp.where(column >= 126, made, result[f, l, 3, top, :])
+        staged[1, f, l, low, :] = jnp.where(column >= 126, half, result[f, l, 3, low, :])
+        if l == 1:
             for side in range(2):
                 lanes = slice(384 * side, 384 * side + 128)
                 copies.append(pltpu.make_async_copy(staged.at[side, f], out.at[f, :, :, lanes], edge_sem.at[side, f]))
@@ -436,7 +445,7 @@
         return pltpu.VMEM((n, 2, tiles, rows, 128), f32)
 
     inputs = [flow_state, colour_map, cell_flags, jnp.transpose(probe_weights, (2, 0, 1))]
-    x_far, x_near, flow, colour, flags, weights = call(
+    x_near, x_far, flow, colour, flags, weights = call(
         pack_x,
         [hbm] * 4,
         [((24, 512), f32, vmem)] * 2 + [(x.shape, x.dtype, vmem) for x in inputs],
@@ -451,11 +460,12 @@
         [banks(6, 4), banks(16, 4), banks(10, 4, 16), banks(10, 4, 16)],
         cost=8000000,
     )(flow, colour, weights)
-    edge, y_far, y_near = call(
+    strip, y_far, y_near = call(
         pack_y,
         [vmem] * 5,
-        [((6, 2, 2, ROWS, 128), f32, vmem), ((24, 128), f32, vmem), ((24, 128), f32, vmem)],
-    )(flow, colour, x_far, x_near, table)
+        [((6, 2, 16, 128), f32, vmem), ((16, 128), f32, vmem), ((16, 128), f32, vmem)],
+        [banks(6, 2)],
+    )(flow, colour, x_near, x_far, table)
     y_far = swap(y_far, "gy", 1)
     y_near = swap(y_near, "gy", 0)
     bank, result = call(
@@ -465,28 +475,28 @@
         [banks(24, 4), banks(10, 4), banks(2, 4, 16), banks(8, 4, 16), pltpu.VMEM((8, 1, 4, 16, 128), f32)],
         alias={4: 0, 5: 1},
         cost=8000000,
-    )(x_far, x_near, table, flags, bank, acc)
+    )(x_near, x_far, table, flags, bank, acc)
     (out,) = call(
         edge_columns,
         [vmem] * 6,
         [((10, 2, 16, 512), f32, hbm)],
         [
             banks(FIELDS, 1),
-            banks(10, 1, 16),
+            banks(10, 1, 8),
             banks(6, 1),
             banks(16, 1),
-            banks(10, 1, 16),
-            banks(10, 1, 16),
+            banks(10, 1, 8),
+            banks(10, 1, 8),
             banks(24, 1),
             banks(10, 1),
-            banks(2, 1, 16),
-            banks(8, 1, 16),
-            pltpu.VMEM((8, 1, 1, 16, 128), f32),
+            banks(2, 1, 8),
+            banks(8, 1, 8),
+            pltpu.VMEM((8, 1, 1, 8, 128), f32),
             pltpu.VMEM((2, 10, 2, 16, 128), f32),
             pltpu.SemaphoreType.DMA((2,)),
             pltpu.SemaphoreType.DMA((2, 10)),
         ],
-    )(y_far, y_near, edge, table, flags, result)
+    )(y_far, y_near, strip, table, flags, result)
     return out.reshape(2, 5, 2, 16, 512)
 
 

time: 20.3 us -> 19.5 us (0.961)
  the two profiles are of different devices: /device:TPU:1 before, /device:TPU:32 now
where the time goes in v5:
time: 19.5 us; the launch traced here: 19.4 us
  starting transfers between devices  12.3 us (63%)
  Pallas kernels  6.86 us (35%)
  waiting for transfers between devices  0.2 us (1%)
    ppermute x4, starting transfers between devices, swap(): return lax.ppermute(value, axis, pairs)  12.3 us
    pallas_call x1, Pallas kernels, local(): call(whole_rows, [vmem] * 6, [(bank.shape, f32, vmem), (acc.shape, f32, v...  2.19 us
    pallas_call x1, Pallas kernels, local(): call(edge_columns, [vmem] * 6, [((10, 2, 16, 512), f32, hbm)], [banks(FIE...  1.72 us
    pallas_call x1, Pallas kernels, local(): call(own_cells, [vmem] * 3, [((FIELDS, 2, 4, ROWS, 128), f32, vmem), ((10...  1.57 us
    pallas_call x1, Pallas kernels, local(): call(pack_x, [hbm] * 4, [((24, 512), f32, vmem)] * 2 + [(x.shape, x.dtype...  1.05 us
  transfers between devices with their start and end apart: 4, of which 1 were waited for; matrix products, arithmetic and copies ran while one was open for 0% of the time, Pallas kernels for 19%

profile of v5, /device:TPU:32, one launch (start us, length us, event | category | flops | bytes accessed | tf_op | source)
XLA Modules:
  0.0 19.4 jit_solution(4991675269268959152)
XLA Ops:
  0.0 1.1 %shard_map.46 = (f32[24,512]{1,0:T(8,128)S(1)}, f32[24,512]{1,0:T(8,128)S(1)}, f32[5,2,16,512]{3,2,1,0:T(8,128)S(1)}, s32[2,16,512]{2,1,0:T(8,128)S(1)}, s32[16,512]{1,0:T(8,128)S(1)}, /*index=5*/f32[5,2,27]{2,1,0:T(2,128)S(1)}) custom-call(f32[5,2,16,512]{3,2,1,0:T(8,128)} %flow.1, s32[2,16,512]{2,1,0:T(8,128)} %colour.1, s32[16,512]{1,0:T(8,128)} %flags.1, ...), custom_call_target="tpu_custom_call" | custom-call | tf_op jit(solution)/shard_map/pallas_call | solution.py:448
  1.1 0.1 collective-permute-start
  1.2 7.7 %collective-permute-start.1 = (f32[24,512]{1,0:T(8,128)S(1)}, f32[24,512]{1,0:T(8,128)S(1)}, u32[]{:S(2)}, u32[]{:S(2)}) collective-permute-start(f32[24,512]{1,0:T(8,128)S(1)} %get-tuple-element.21), channel_id=1, source_target_pairs={{8,16},{16,8},{24,32},{32,24},{40,48},{48,40},{56,64},{64,56},{72,... | collective-permute-start | bytes 147464 | tf_op jit(solution)/shard_map/ppermute | solution.py:424
  8.9 1.6 %shard_map.47 = (f32[39,2,4,40,128]{4,3,2,1,0:T(8,128)S(1)}, f32[10,2,4,16,128]{4,3,2,1,0:T(8,128)S(1)}, f32[16,128]{1,0:T(8,128)S(1)}) custom-call(f32[5,2,16,512]{3,2,1,0:T(8,128)S(1)} %get-tuple-element.18.flow, s32[2,16,512]{2,1,0:T(8,128)S(1)} %get-tuple-element.19.colour, f32[5,2,27]{2,1,0:T(2,128)S(1)} %get-tuple-element.22.weights), custom_call_target="tpu_custom_call" | custom-call | flops 8000000 | bytes 8000000 | tf_op jit(solution)/shard_map/pallas_call | solution.py:456
  10.4 0.0 collective-permute-done.near
  10.5 0.2 collective-permute-done.1.far
  10.6 0.3 %shard_map.48 = (f32[6,2,16,128]{3,2,1,0:T(8,128)S(1)}, f32[16,128]{1,0:T(8,128)S(1)}, f32[16,128]{1,0:T(8,128)S(1)}) custom-call(f32[5,2,16,512]{3,2,1,0:T(8,128)S(1)} %get-tuple-element.18.flow, s32[2,16,512]{2,1,0:T(8,128)S(1)} %get-tuple-element.19.colour, f32[24,512]{1,0:T(8,128)S(1)} %collective-permute-done.near, ...), custom_call_target="tpu_custom_call" | custom-call | tf_op jit(solution)/shard_map/pallas_call | solution.py:463
  11.0 2.1 %collective-permute-start.2 = (f32[16,128]{1,0:T(8,128)S(1)}, f32[16,128]{1,0:T(8,128)S(1)}, u32[]{:S(2)}, u32[]{:S(2)}) collective-permute-start(f32[16,128]{1,0:T(8,128)S(1)} %get-tuple-element.24), channel_id=1, source_target_pairs={{1,2},{2,1},{3,4},{4,3},{5,6},{6,5},{7,0},{0,7},{9,10},{10,9},{11,... | collective-permute-start | bytes 24584 | tf_op jit(solution)/shard_map/ppermute | solution.py:424
  13.1 2.4 %collective-permute-start.3 = (f32[16,128]{1,0:T(8,128)S(1)}, f32[16,128]{1,0:T(8,128)S(1)}, u32[]{:S(2)}, u32[]{:S(2)}) collective-permute-start(f32[16,128]{1,0:T(8,128)S(1)} %get-tuple-element.25), channel_id=1, source_target_pairs={{0,1},{1,0},{2,3},{3,2},{4,5},{5,4},{6,7},{7,6},{8,9},{9,8},{10,11... | collective-permute-start | bytes 24584 | tf_op jit(solution)/shard_map/ppermute | solution.py:424
  15.5 2.2 %shard_map.49 = (f32[39,2,4,40,128]{4,3,2,1,0:T(8,128)S(1)}, f32[10,2,4,16,128]{4,3,2,1,0:T(8,128)S(1)}) custom-call(f32[24,512]{1,0:T(8,128)S(1)} %collective-permute-done.near, f32[24,512]{1,0:T(8,128)S(1)} %collective-permute-done.1.far, f32[16,128]{1,0:T(8,128)S(1)} %get-tuple-element.23.table, ...), custom_call_target="tpu_custom_call", output_to_operand_aliasing={{0}: (4, {}), {1}: (5, {})} | custom-call | flops 8000000 | bytes 8000000 | tf_op jit(solution)/shard_map/pallas_call | solution.py:471
  17.7 0.0 collective-permute-done.2.far
  17.7 0.0 collective-permute-done.3.near
  17.7 1.7 %shard_map.50 = f32[10,2,16,512]{3,2,1,0:T(8,128)} custom-call(f32[16,128]{1,0:T(8,128)S(1)} %collective-permute-done.2.far, f32[16,128]{1,0:T(8,128)S(1)} %collective-permute-done.3.near, f32[6,2,16,128]{3,2,1,0:T(8,128)S(1)} %get-tuple-element.26.strip, f32[16,128]{1,0:T(8,128)S(1)} %get-tuple-element.23.table, s32[16,512]{1,0:T(8,128)S(1)} %get-tuple-element.27.flags, ...), custom_call_target="tpu_custom_call" | custom-call | tf_op jit(solution)/shard_map/pallas_call | solution.py:479
Async XLA Ops:
  1.1 9.4 %collective-permute-start = (f32[24,512]{1,0:T(8,128)S(1)}, f32[24,512]{1,0:T(8,128)S(1)}, u32[]{:S(2)}, u32[]{:S(2)}) collective-permute-start(f32[24,512]{1,0:T(8,128)S(1)} %get-tuple-element.20), channel_id=1, source_target_pairs={{0,8},{8,0},{16,24},{24,16},{32,40},{40,32},{48,56},{56,48},{64,72... | collective-permute-start | bytes 147464 | tf_op jit(solution)/shard_map/ppermute | solution.py:424
  1.2 9.5 %collective-permute-start.1 = (f32[24,512]{1,0:T(8,128)S(1)}, f32[24,512]{1,0:T(8,128)S(1)}, u32[]{:S(2)}, u32[]{:S(2)}) collective-permute-start(f32[24,512]{1,0:T(8,128)S(1)} %get-tuple-element.21), channel_id=1, source_target_pairs={{8,16},{16,8},{24,32},{32,24},{40,48},{48,40},{56,64},{64,56},{72,... | collective-permute-start | bytes 147464 | tf_op jit(solution)/shard_map/ppermute | solution.py:424
  11.0 6.7 %collective-permute-start.2 = (f32[16,128]{1,0:T(8,128)S(1)}, f32[16,128]{1,0:T(8,128)S(1)}, u32[]{:S(2)}, u32[]{:S(2)}) collective-permute-start(f32[16,128]{1,0:T(8,128)S(1)} %get-tuple-element.24), channel_id=1, source_target_pairs={{1,2},{2,1},{3,4},{4,3},{5,6},{6,5},{7,0},{0,7},{9,10},{10,9},{11,... | collective-permute-start | bytes 24584 | tf_op jit(solution)/shard_map/ppermute | solution.py:424
  13.1 4.6 %collective-permute-start.3 = (f32[16,128]{1,0:T(8,128)S(1)}, f32[16,128]{1,0:T(8,128)S(1)}, u32[]{:S(2)}, u32[]{:S(2)}) collective-permute-start(f32[16,128]{1,0:T(8,128)S(1)} %get-tuple-element.25), channel_id=1, source_target_pairs={{0,1},{1,0},{2,3},{3,2},{4,5},{5,4},{6,7},{7,6},{8,9},{9,8},{10,11... | collective-permute-start | bytes 24584 | tf_op jit(solution)/shard_map/ppermute | solution.py:424

commit v6 on v5

--- a/solution.py
+++ b/solution.py
@@ -13,14 +13,14 @@
 TENSOR = ((0, 1, 2), (1, 3, 4), (2, 4, 5))
 
 
-def get(ref, f, l, row):
-    tiles = [ref[f, l, c, row : row + 8, :] for c in range(ref.shape[2])]
+def get(ref, f, l, row, height=8):
+    tiles = [ref[f, l, c, row : row + height, :] for c in range(ref.shape[2])]
     return tiles[0] if len(tiles) == 1 else jnp.concatenate(tiles, axis=1)
 
 
 def put(ref, f, l, row, value):
     for c in range(ref.shape[2]):
-        ref[f, l, c, row : row + 8, :] = value[:, 128 * c : 128 * c + 128]
+        ref[f, l, c, row : row + value.shape[0], :] = value[:, 128 * c : 128 * c + 128]
 
 
 def ahead(value, step=1):
@@ -132,16 +132,16 @@
                     put(acc, 5 * p + v, l, 8 * t, made + wall if l == 1 else made - wall)
 
 
-def stresses(bank, stress, rows):
+def stresses(bank, stress, rows, height=8):
     quarter = 0.25 * MU
     for row in rows:
         for k in range(3):
             q = PRIM + 4 * k
-            grad_z = [2.0 * (get(bank, q + i, 1, row) - get(bank, q + i, 0, row)) for i in range(4 if k else 3)]
+            grad_z = [2.0 * (get(bank, q + i, 1, row, height) - get(bank, q + i, 0, row, height)) for i in range(4 if k else 3)]
             for l in range(2):
                 count = range(4 if k else 3)
-                grad_x = [get(bank, q + i, l, row + 1) - get(bank, q + i, l, row - 1) for i in count]
-                here = [get(bank, q + i, l, row) for i in count]
+                grad_x = [get(bank, q + i, l, row + 1, height) - get(bank, q + i, l, row - 1, height) for i in count]
+                here = [get(bank, q + i, l, row, height) for i in count]
                 grad_y = [ahead(h, 1) - ahead(h, -1) for h in here]
                 third = (2.0 / 3.0) * (grad_x[0] + grad_y[1] + grad_z[2])
                 base = 9 * k - 3 if k else 0
@@ -157,17 +157,17 @@
                     put(stress, base + 8, l, row, (0.25 * KAPPA) * grad_z[3])
 
 
-def x_faces(bank, stress, xface, rows):
+def x_faces(bank, stress, xface, rows, height=8):
     for l in range(2):
         for row in rows:
-            pair = lambda ref, f: get(ref, f, l, row) + get(ref, f, l, row + 1)
+            pair = lambda ref, f: get(ref, f, l, row, height) + get(ref, f, l, row + 1, height)
             s_sum = pair(bank, SPEED)
             ds = [pair(bank, SPEED + 1 + p) for p in range(2)]
             for v in range(5):
-                jump = get(bank, STATE + v, l, row + 1) - get(bank, STATE + v, l, row)
+                jump = get(bank, STATE + v, l, row + 1, height) - get(bank, STATE + v, l, row, height)
                 for p in range(2):
                     f = SEED + 5 * p + v
-                    made = ds[p] * jump + s_sum * (get(bank, f, l, row + 1) - get(bank, f, l, row))
+                    made = ds[p] * jump + s_sum * (get(bank, f, l, row + 1, height) - get(bank, f, l, row, height))
                     if v == 4:
                         work = 0.0
                         for e in range(3):
@@ -279,20 +279,12 @@
 def x_halo(near, far, store):
     odd = lax.rem(lax.axis_index("gx"), 2)
 
-    def fill(src, row):
+    low = jnp.where(odd == 0, far[...], near[...])
+    high = jnp.where(odd == 0, near[...], far[...])
+    for src, row in ((low, BASE - 2), (high, BASE + 16)):
         for l in range(2):
             for v in range(6):
                 store(v, l, row, src, 4 * v + 2 * l)
-
-    @pl.when(odd == 0)
-    def _():
-        fill(far, BASE - 2)
-        fill(near, BASE + 16)
-
-    @pl.when(odd == 1)
-    def _():
-        fill(near, BASE - 2)
-        fill(far, BASE + 16)
 
 
 def fold(first, last):
@@ -315,33 +307,26 @@
             edge[v, l, side, row : row + 2, :] = src[at : at + 2, 384 * side : 384 * side + 128]
 
     x_halo(near, far, store)
-    lane = lax.broadcasted_iota(jnp.int32, (24, 128), 1)
-
-    def columns(side, first):
-        made = jnp.zeros((24, 128), jnp.float32)
+    for v in range(6):
+        for l in range(2):
+            span = slice(BASE - 4, BASE + 20)
+            strip[v, l] = fold(edge[v, l, 0, span, :], edge[v, l, 1, span, :])
+    lane = lax.broadcasted_iota(jnp.int32, (16, 128), 1) & 63
+
+    def columns(first):
+        made = jnp.zeros((16, 128), jnp.float32)
         for l in range(2):
             for v in range(6):
                 at = 2 * (6 * l + v)
-                moved = pltpu.roll(edge[v, l, side, BASE - 4 : BASE + 20, :], (at - first) % 128, 1)
+                moved = pltpu.roll(strip[v, l], (at - first) % 128, 1)
                 made = jnp.where((lane >= at) & (lane < at + 2), moved, made)
-        return jnp.where(lane[:16] < 64, made[:16], pltpu.roll(made[8:], 64, 1))
-
-    for v in range(6):
-        for l in range(2):
-            span = slice(BASE - 4, BASE + 20)
-            strip[v, l] = fold(edge[v, l, 0, span, :], edge[v, l, 1, span, :])
-    left, right = columns(0, 0), columns(1, 126)
+        return made
+
+    left, right = columns(32), columns(126)
     odd = lax.rem(lax.axis_index("gy"), 2)
 
-    @pl.when(odd == 0)
-    def _():
-        to_near[...] = right
-        to_far[...] = left
-
-    @pl.when(odd == 1)
-    def _():
-        to_near[...] = left
-        to_far[...] = right
+    to_near[...] = jnp.where(odd == 0, right, left)
+    to_far[...] = jnp.where(odd == 0, left, right)
 
 
 def whole_rows(near, far, table, flags, bank_in, acc, bank, result, stress, xface, yface, ypart, zface):
@@ -372,27 +357,19 @@
     place = lane & 63
     odd = lax.rem(lax.axis_index("gy"), 2)
 
-    def unpack(low, high):
-        for l in range(2):
-            for v in range(6):
-                at = 2 * (6 * l + v)
-                made = jnp.where(place < 2, pltpu.roll(high[...], (-at) % 128, 1), strip[v, l])
-                made = jnp.where((place == 30) | (place == 31), pltpu.roll(low[...], 30 - at, 1), made)
-                bank[STATE + v, l, 0, BASE - 4 : BASE + 12, :] = made
-
-    @pl.when(odd == 0)
-    def _():
-        unpack(far, near)
-
-    @pl.when(odd == 1)
-    def _():
-        unpack(near, far)
-
-    rows = (BASE - 4, BASE + 4)
+    low = jnp.where(odd == 0, far[...], near[...])
+    high = jnp.where(odd == 0, near[...], far[...])
+    for l in range(2):
+        for v in range(6):
+            at = 2 * (6 * l + v)
+            made = jnp.where(place < 2, pltpu.roll(high, (-at) % 128, 1), strip[v, l])
+            made = jnp.where((place == 30) | (place == 31), pltpu.roll(low, 30 - at, 1), made)
+            bank[STATE + v, l, 0, BASE - 4 : BASE + 12, :] = made
+
     pointwise(bank, table, (BASE - 4,), 16, speed_yz, flux_yz)
     inviscid_yz(bank, speed_yz, flux_yz, cell, face, acc)
-    stresses(bank, stress, rows)
-    x_faces(bank, stress, xface, rows)
+    stresses(bank, stress, (BASE - 4,), 16)
+    x_faces(bank, stress, xface, (BASE - 4,), 16)
     column = lane[:8]
     solid = lambda row: fold(flags[:, 0:128], flags[:, 384:512])
     copies = []

time: 19.5 us -> 19.4 us (level)
  no operation moved by 1% of the time
where the time goes in v6:
time: 19.4 us; the launch traced here: 19.3 us
  starting transfers between devices  12.4 us (64%)
  Pallas kernels  6.73 us (35%)
  waiting for transfers between devices  0.2 us (1%)
    ppermute x4, starting transfers between devices, swap(): return lax.ppermute(value, axis, pairs)  12.4 us
    pallas_call x1, Pallas kernels, local(): call(whole_rows, [vmem] * 6, [(bank.shape, f32, vmem), (acc.shape, f32, v...  2.18 us
    pallas_call x1, Pallas kernels, local(): call(edge_columns, [vmem] * 6, [((10, 2, 16, 512), f32, hbm)], [banks(FIE...  1.64 us
    pallas_call x1, Pallas kernels, local(): call(own_cells, [vmem] * 3, [((FIELDS, 2, 4, ROWS, 128), f32, vmem), ((10...  1.57 us
    pallas_call x1, Pallas kernels, local(): call(pack_x, [hbm] * 4, [((24, 512), f32, vmem)] * 2 + [(x.shape, x.dtype...  1.05 us
  transfers between devices with their start and end apart: 4, of which 1 were waited for; matrix products, arithmetic and copies ran while one was open for 0% of the time, Pallas kernels for 19%

profile of v6, /device:TPU:32, one launch (start us, length us, event | category | flops | bytes accessed | tf_op | source)
XLA Modules:
  0.0 19.3 jit_solution(4616582320397237551)
XLA Ops:
  0.0 1.1 %shard_map.46 = (f32[24,512]{1,0:T(8,128)S(1)}, f32[24,512]{1,0:T(8,128)S(1)}, f32[5,2,16,512]{3,2,1,0:T(8,128)S(1)}, s32[2,16,512]{2,1,0:T(8,128)S(1)}, s32[16,512]{1,0:T(8,128)S(1)}, /*index=5*/f32[5,2,27]{2,1,0:T(2,128)S(1)}) custom-call(f32[5,2,16,512]{3,2,1,0:T(8,128)} %flow.1, s32[2,16,512]{2,1,0:T(8,128)} %colour.1, s32[16,512]{1,0:T(8,128)} %flags.1, ...), custom_call_target="tpu_custom_call" | custom-call | tf_op jit(solution)/shard_map/pallas_call | solution.py:425
  1.1 0.1 collective-permute-start
  1.2 7.7 %collective-permute-start.1 = (f32[24,512]{1,0:T(8,128)S(1)}, f32[24,512]{1,0:T(8,128)S(1)}, u32[]{:S(2)}, u32[]{:S(2)}) collective-permute-start(f32[24,512]{1,0:T(8,128)S(1)} %get-tuple-element.21), channel_id=1, source_target_pairs={{8,16},{16,8},{24,32},{32,24},{40,48},{48,40},{56,64},{64,56},{72,... | collective-permute-start | bytes 147464 | tf_op jit(solution)/shard_map/ppermute | solution.py:401
  8.9 1.6 %shard_map.47 = (f32[39,2,4,40,128]{4,3,2,1,0:T(8,128)S(1)}, f32[10,2,4,16,128]{4,3,2,1,0:T(8,128)S(1)}, f32[16,128]{1,0:T(8,128)S(1)}) custom-call(f32[5,2,16,512]{3,2,1,0:T(8,128)S(1)} %get-tuple-element.18.flow, s32[2,16,512]{2,1,0:T(8,128)S(1)} %get-tuple-element.19.colour, f32[5,2,27]{2,1,0:T(2,128)S(1)} %get-tuple-element.22.weights), custom_call_target="tpu_custom_call" | custom-call | flops 8000000 | bytes 8000000 | tf_op jit(solution)/shard_map/pallas_call | solution.py:433
  10.4 0.0 collective-permute-done.near
  10.5 0.2 %collective-permute-done.1.far = f32[24,512]{1,0:T(8,128)S(1)} collective-permute-done((f32[24,512]{1,0:T(8,128)S(1)}, f32[24,512]{1,0:T(8,128)S(1)}, u32[]{:S(2)}, u32[]{:S(2)}) %collective-permute-start.1) | collective-permute-done | bytes 49184 | tf_op jit(solution)/shard_map/ppermute | solution.py:401
  10.6 0.3 %shard_map.48 = (f32[6,2,16,128]{3,2,1,0:T(8,128)S(1)}, f32[16,128]{1,0:T(8,128)S(1)}, f32[16,128]{1,0:T(8,128)S(1)}) custom-call(f32[5,2,16,512]{3,2,1,0:T(8,128)S(1)} %get-tuple-element.18.flow, s32[2,16,512]{2,1,0:T(8,128)S(1)} %get-tuple-element.19.colour, f32[24,512]{1,0:T(8,128)S(1)} %collective-permute-done.near, ...), custom_call_target="tpu_custom_call" | custom-call | tf_op jit(solution)/shard_map/pallas_call | solution.py:440
  10.9 2.2 %collective-permute-start.2 = (f32[16,128]{1,0:T(8,128)S(1)}, f32[16,128]{1,0:T(8,128)S(1)}, u32[]{:S(2)}, u32[]{:S(2)}) collective-permute-start(f32[16,128]{1,0:T(8,128)S(1)} %get-tuple-element.24), channel_id=1, source_target_pairs={{1,2},{2,1},{3,4},{4,3},{5,6},{6,5},{7,0},{0,7},{9,10},{10,9},{11,... | collective-permute-start | bytes 24584 | tf_op jit(solution)/shard_map/ppermute | solution.py:401
  13.1 2.4 %collective-permute-start.3 = (f32[16,128]{1,0:T(8,128)S(1)}, f32[16,128]{1,0:T(8,128)S(1)}, u32[]{:S(2)}, u32[]{:S(2)}) collective-permute-start(f32[16,128]{1,0:T(8,128)S(1)} %get-tuple-element.25), channel_id=1, source_target_pairs={{0,1},{1,0},{2,3},{3,2},{4,5},{5,4},{6,7},{7,6},{8,9},{9,8},{10,11... | collective-permute-start | bytes 24584 | tf_op jit(solution)/shard_map/ppermute | solution.py:401
  15.5 2.2 %shard_map.49 = (f32[39,2,4,40,128]{4,3,2,1,0:T(8,128)S(1)}, f32[10,2,4,16,128]{4,3,2,1,0:T(8,128)S(1)}) custom-call(f32[24,512]{1,0:T(8,128)S(1)} %collective-permute-done.near, f32[24,512]{1,0:T(8,128)S(1)} %collective-permute-done.1.far, f32[16,128]{1,0:T(8,128)S(1)} %get-tuple-element.23.table, ...), custom_call_target="tpu_custom_call", output_to_operand_aliasing={{0}: (4, {}), {1}: (5, {})} | custom-call | flops 8000000 | bytes 8000000 | tf_op jit(solution)/shard_map/pallas_call | solution.py:448
  17.7 0.0 collective-permute-done.2.far
  17.7 0.0 collective-permute-done.3.near
  17.7 1.6 %shard_map.50 = f32[10,2,16,512]{3,2,1,0:T(8,128)} custom-call(f32[16,128]{1,0:T(8,128)S(1)} %collective-permute-done.2.far, f32[16,128]{1,0:T(8,128)S(1)} %collective-permute-done.3.near, f32[6,2,16,128]{3,2,1,0:T(8,128)S(1)} %get-tuple-element.26.strip, f32[16,128]{1,0:T(8,128)S(1)} %get-tuple-element.23.table, s32[16,512]{1,0:T(8,128)S(1)} %get-tuple-element.27.flags, ...), custom_call_target="tpu_custom_call" | custom-call | tf_op jit(solution)/shard_map/pallas_call | solution.py:456
Async XLA Ops:
  1.1 9.4 %collective-permute-start = (f32[24,512]{1,0:T(8,128)S(1)}, f32[24,512]{1,0:T(8,128)S(1)}, u32[]{:S(2)}, u32[]{:S(2)}) collective-permute-start(f32[24,512]{1,0:T(8,128)S(1)} %get-tuple-element.20), channel_id=1, source_target_pairs={{0,8},{8,0},{16,24},{24,16},{32,40},{40,32},{48,56},{56,48},{64,72... | collective-permute-start | bytes 147464 | tf_op jit(solution)/shard_map/ppermute | solution.py:401
  1.2 9.5 %collective-permute-start.1 = (f32[24,512]{1,0:T(8,128)S(1)}, f32[24,512]{1,0:T(8,128)S(1)}, u32[]{:S(2)}, u32[]{:S(2)}) collective-permute-start(f32[24,512]{1,0:T(8,128)S(1)} %get-tuple-element.21), channel_id=1, source_target_pairs={{8,16},{16,8},{24,32},{32,24},{40,48},{48,40},{56,64},{64,56},{72,... | collective-permute-start | bytes 147464 | tf_op jit(solution)/shard_map/ppermute | solution.py:401
  10.9 6.8 %collective-permute-start.2 = (f32[16,128]{1,0:T(8,128)S(1)}, f32[16,128]{1,0:T(8,128)S(1)}, u32[]{:S(2)}, u32[]{:S(2)}) collective-permute-start(f32[16,128]{1,0:T(8,128)S(1)} %get-tuple-element.24), channel_id=1, source_target_pairs={{1,2},{2,1},{3,4},{4,3},{5,6},{6,5},{7,0},{0,7},{9,10},{10,9},{11,... | collective-permute-start | bytes 24584 | tf_op jit(solution)/shard_map/ppermute | solution.py:401
  13.1 4.6 %collective-permute-start.3 = (f32[16,128]{1,0:T(8,128)S(1)}, f32[16,128]{1,0:T(8,128)S(1)}, u32[]{:S(2)}, u32[]{:S(2)}) collective-permute-start(f32[16,128]{1,0:T(8,128)S(1)} %get-tuple-element.25), channel_id=1, source_target_pairs={{0,1},{1,0},{2,3},{3,2},{4,5},{5,4},{6,7},{7,6},{8,9},{9,8},{10,11... | collective-permute-start | bytes 24584 | tf_op jit(solution)/shard_map/ppermute | solution.py:401

commit v7 on v6

--- a/solution.py
+++ b/solution.py
@@ -294,7 +294,7 @@
     return jnp.where((lane[:rows] >= 48) & (lane[:rows] < 112), pltpu.roll(made[8:], 64, 1), made[:rows])
 
 
-def pack_y(flow, colour, near, far, table, strip, to_far, to_near, edge):
+def pack_y(flow, colour, near, far, table, strip, to_near, to_far, edge):
     for l in range(2):
         for side in range(2):
             lanes = slice(384 * side, 384 * side + 128)
@@ -345,7 +345,7 @@
 
 
 def edge_columns(
-    far, near, strip, table, flags, result, out, bank, acc, speed_yz, flux_yz, cell, face, stress, xface, yface, ypart,
+    near, far, strip, table, flags, result, out, bank, acc, speed_yz, flux_yz, cell, face, stress, xface, yface, ypart,
     zface, staged, middle_sem, edge_sem,
 ):
     middle = []
@@ -437,7 +437,7 @@
         [banks(6, 4), banks(16, 4), banks(10, 4, 16), banks(10, 4, 16)],
         cost=8000000,
     )(flow, colour, weights)
-    strip, y_far, y_near = call(
+    strip, y_near, y_far = call(
         pack_y,
         [vmem] * 5,
         [((6, 2, 16, 128), f32, vmem), ((16, 128), f32, vmem), ((16, 128), f32, vmem)],
@@ -473,7 +473,7 @@
             pltpu.SemaphoreType.DMA((2,)),
             pltpu.SemaphoreType.DMA((2, 10)),
         ],
-    )(y_far, y_near, strip, table, flags, result)
+    )(y_near, y_far, strip, table, flags, result)
     return out.reshape(2, 5, 2, 16, 512)
 
 

time: 19.4 us -> 19.6 us (1.010)
  the two profiles are of different devices: /device:TPU:32 before, /device:TPU:56 now
where the time goes in v7:
time: 19.6 us; the launch traced here: 19.5 us
  starting transfers between devices  9.56 us (49%)
  Pallas kernels  6.72 us (34%)
  waiting for transfers between devices  3.15 us (16%)
    ppermute x4, starting transfers between devices, swap(): return lax.ppermute(value, axis, pairs)  9.56 us
    ppermute x4, waiting for transfers between devices, swap(): return lax.ppermute(value, axis, pairs)  3.15 us
    pallas_call x1, Pallas kernels, local(): call(whole_rows, [vmem] * 6, [(bank.shape, f32, vmem), (acc.shape, f32, v...  2.18 us
    pallas_call x1, Pallas kernels, local(): call(edge_columns, [vmem] * 6, [((10, 2, 16, 512), f32, hbm)], [banks(FIE...  1.62 us
    pallas_call x1, Pallas kernels, local(): call(own_cells, [vmem] * 3, [((FIELDS, 2, 4, ROWS, 128), f32, vmem), ((10...  1.57 us
    pallas_call x1, Pallas kernels, local(): call(pack_x, [hbm] * 4, [((24, 512), f32, vmem)] * 2 + [(x.shape, x.dtype...  1.05 us
  transfers between devices with their start and end apart: 4, of which 2 were waited for; matrix products, arithmetic and copies ran while one was open for 0% of the time, Pallas kernels for 19%

profile of v7, /device:TPU:56, one launch (start us, length us, event | category | flops | bytes accessed | tf_op | source)
XLA Modules:
  0.0 19.5 jit_solution(16443702865672143365)
XLA Ops:
  0.0 1.1 %shard_map.46 = (f32[24,512]{1,0:T(8,128)S(1)}, f32[24,512]{1,0:T(8,128)S(1)}, f32[5,2,16,512]{3,2,1,0:T(8,128)S(1)}, s32[2,16,512]{2,1,0:T(8,128)S(1)}, s32[16,512]{1,0:T(8,128)S(1)}, /*index=5*/f32[5,2,27]{2,1,0:T(2,128)S(1)}) custom-call(f32[5,2,16,512]{3,2,1,0:T(8,128)} %flow.1, s32[2,16,512]{2,1,0:T(8,128)} %colour.1, s32[16,512]{1,0:T(8,128)} %flags.1, ...), custom_call_target="tpu_custom_call" | custom-call | tf_op jit(solution)/shard_map/pallas_call | solution.py:425
  1.1 0.1 collective-permute-start
  1.2 7.7 %collective-permute-start.1 = (f32[24,512]{1,0:T(8,128)S(1)}, f32[24,512]{1,0:T(8,128)S(1)}, u32[]{:S(2)}, u32[]{:S(2)}) collective-permute-start(f32[24,512]{1,0:T(8,128)S(1)} %get-tuple-element.21), channel_id=1, source_target_pairs={{8,16},{16,8},{24,32},{32,24},{40,48},{48,40},{56,64},{64,56},{72,... | collective-permute-start | bytes 147464 | tf_op jit(solution)/shard_map/ppermute | solution.py:401
  8.9 1.6 %shard_map.47 = (f32[39,2,4,40,128]{4,3,2,1,0:T(8,128)S(1)}, f32[10,2,4,16,128]{4,3,2,1,0:T(8,128)S(1)}, f32[16,128]{1,0:T(8,128)S(1)}) custom-call(f32[5,2,16,512]{3,2,1,0:T(8,128)S(1)} %get-tuple-element.18.flow, s32[2,16,512]{2,1,0:T(8,128)S(1)} %get-tuple-element.19.colour, f32[5,2,27]{2,1,0:T(2,128)S(1)} %get-tuple-element.22.weights), custom_call_target="tpu_custom_call" | custom-call | flops 8000000 | bytes 8000000 | tf_op jit(solution)/shard_map/pallas_call | solution.py:433
  10.4 0.0 collective-permute-done.near
  10.5 0.2 collective-permute-done.1.far
  10.6 0.3 %shard_map.48 = (f32[6,2,16,128]{3,2,1,0:T(8,128)S(1)}, f32[16,128]{1,0:T(8,128)S(1)}, f32[16,128]{1,0:T(8,128)S(1)}) custom-call(f32[5,2,16,512]{3,2,1,0:T(8,128)S(1)} %get-tuple-element.18.flow, s32[2,16,512]{2,1,0:T(8,128)S(1)} %get-tuple-element.19.colour, f32[24,512]{1,0:T(8,128)S(1)} %collective-permute-done.near, ...), custom_call_target="tpu_custom_call" | custom-call | tf_op jit(solution)/shard_map/pallas_call | solution.py:440
  10.9 1.2 %collective-permute-start.2 = (f32[16,128]{1,0:T(8,128)S(1)}, f32[16,128]{1,0:T(8,128)S(1)}, u32[]{:S(2)}, u32[]{:S(2)}) collective-permute-start(f32[16,128]{1,0:T(8,128)S(1)} %get-tuple-element.24), channel_id=1, source_target_pairs={{0,1},{1,0},{2,3},{3,2},{4,5},{5,4},{6,7},{7,6},{8,9},{9,8},{10,11... | collective-permute-start | bytes 24584 | tf_op jit(solution)/shard_map/ppermute | solution.py:401
  12.1 0.6 %collective-permute-start.3 = (f32[16,128]{1,0:T(8,128)S(1)}, f32[16,128]{1,0:T(8,128)S(1)}, u32[]{:S(2)}, u32[]{:S(2)}) collective-permute-start(f32[16,128]{1,0:T(8,128)S(1)} %get-tuple-element.25), channel_id=1, source_target_pairs={{1,2},{2,1},{3,4},{4,3},{5,6},{6,5},{7,0},{0,7},{9,10},{10,9},{11,... | collective-permute-start | bytes 24584 | tf_op jit(solution)/shard_map/ppermute | solution.py:401
  12.7 2.2 %shard_map.49 = (f32[39,2,4,40,128]{4,3,2,1,0:T(8,128)S(1)}, f32[10,2,4,16,128]{4,3,2,1,0:T(8,128)S(1)}) custom-call(f32[24,512]{1,0:T(8,128)S(1)} %collective-permute-done.near, f32[24,512]{1,0:T(8,128)S(1)} %collective-permute-done.1.far, f32[16,128]{1,0:T(8,128)S(1)} %get-tuple-element.23.table, ...), custom_call_target="tpu_custom_call", output_to_operand_aliasing={{0}: (4, {}), {1}: (5, {})} | custom-call | flops 8000000 | bytes 8000000 | tf_op jit(solution)/shard_map/pallas_call | solution.py:448
  14.9 0.0 collective-permute-done.2.near
  14.9 3.0 %collective-permute-done.3.far = f32[16,128]{1,0:T(8,128)S(1)} collective-permute-done((f32[16,128]{1,0:T(8,128)S(1)}, f32[16,128]{1,0:T(8,128)S(1)}, u32[]{:S(2)}, u32[]{:S(2)}) %collective-permute-start.3) | collective-permute-done | bytes 8224 | tf_op jit(solution)/shard_map/ppermute | solution.py:401
  17.9 1.6 %shard_map.50 = f32[10,2,16,512]{3,2,1,0:T(8,128)} custom-call(f32[16,128]{1,0:T(8,128)S(1)} %collective-permute-done.2.near, f32[16,128]{1,0:T(8,128)S(1)} %collective-permute-done.3.far, f32[6,2,16,128]{3,2,1,0:T(8,128)S(1)} %get-tuple-element.26.strip, f32[16,128]{1,0:T(8,128)S(1)} %get-tuple-element.23.table, s32[16,512]{1,0:T(8,128)S(1)} %get-tuple-element.27.flags, ...), custom_call_target="tpu_custom_call" | custom-call | tf_op jit(solution)/shard_map/pallas_call | solution.py:456
Async XLA Ops:
  1.1 9.4 %collective-permute-start = (f32[24,512]{1,0:T(8,128)S(1)}, f32[24,512]{1,0:T(8,128)S(1)}, u32[]{:S(2)}, u32[]{:S(2)}) collective-permute-start(f32[24,512]{1,0:T(8,128)S(1)} %get-tuple-element.20), channel_id=1, source_target_pairs={{0,8},{8,0},{16,24},{24,16},{32,40},{40,32},{48,56},{56,48},{64,72... | collective-permute-start | bytes 147464 | tf_op jit(solution)/shard_map/ppermute | solution.py:401
  1.2 9.5 %collective-permute-start.1 = (f32[24,512]{1,0:T(8,128)S(1)}, f32[24,512]{1,0:T(8,128)S(1)}, u32[]{:S(2)}, u32[]{:S(2)}) collective-permute-start(f32[24,512]{1,0:T(8,128)S(1)} %get-tuple-element.21), channel_id=1, source_target_pairs={{8,16},{16,8},{24,32},{32,24},{40,48},{48,40},{56,64},{64,56},{72,... | collective-permute-start | bytes 147464 | tf_op jit(solution)/shard_map/ppermute | solution.py:401
  10.9 4.0 %collective-permute-start.2 = (f32[16,128]{1,0:T(8,128)S(1)}, f32[16,128]{1,0:T(8,128)S(1)}, u32[]{:S(2)}, u32[]{:S(2)}) collective-permute-start(f32[16,128]{1,0:T(8,128)S(1)} %get-tuple-element.24), channel_id=1, source_target_pairs={{0,1},{1,0},{2,3},{3,2},{4,5},{5,4},{6,7},{7,6},{8,9},{9,8},{10,11... | collective-permute-start | bytes 24584 | tf_op jit(solution)/shard_map/ppermute | solution.py:401
  12.1 5.8 %collective-permute-start.3 = (f32[16,128]{1,0:T(8,128)S(1)}, f32[16,128]{1,0:T(8,128)S(1)}, u32[]{:S(2)}, u32[]{:S(2)}) collective-permute-start(f32[16,128]{1,0:T(8,128)S(1)} %get-tuple-element.25), channel_id=1, source_target_pairs={{1,2},{2,1},{3,4},{4,3},{5,6},{6,5},{7,0},{0,7},{9,10},{10,9},{11,... | collective-permute-start | bytes 24584 | tf_op jit(solution)/shard_map/ppermute | solution.py:401
